TPU v7x, 32 devices: a whole 2x2x4 slice. The times are simulated.
32 devices in a mesh: section: 2 (over core), tm: 8 (over z, x), tile: 2 (over y).
Axes of the slice: x: 2, y: 2, z: 4, core: 2. Of those that a mesh axis runs over, the one named last changes fastest.
Arguments:
- features: bfloat16 [16, 16, 64, 256], P('tm', 'tile', None, 'section'), may hold values from -320 to 320
- norm_gain_in: float32 [256], replicated, may hold values from 0.1 to 1.9
- norm_shift_in: float32 [256], replicated, may hold values from -0.8 to 0.8
- conv_in_weight: bfloat16 [3, 3, 3, 256, 128], replicated, may hold values from -0.078125 to 0.078125
- conv_in_bias: float32 [128], replicated, may hold values from -1 to 1
- norm_gain_mid: float32 [128], replicated, may hold values from 0.1 to 1.9
- norm_shift_mid: float32 [128], replicated, may hold values from -0.8 to 0.8
- conv_mid_weight: bfloat16 [3, 3, 3, 128, 128], replicated, may hold values from -0.109375 to 0.109375
- conv_mid_bias: float32 [128], replicated, may hold values from -0.6 to 0.6
- skip_weight: bfloat16 [256, 128], replicated, may hold values from -0.09375 to 0.09375
- skip_bias: float32 [128], replicated, may hold values from -0.6 to 0.6
Outputs:
- block_out: bfloat16 [16, 16, 64, 128], P('tm', 'tile', 'section')
All inputs are finite; a program needn't handle non-finite values.
Results may differ from a plain program's by a relative error of at most 0.008.
Values may be sent and summed in bfloat16 or wider, within the bound.
No kernel may reach another device: no remote copies, remote signals or barrier semaphores. Data moves between devices by JAX's collectives and lax.ppermute only.
A program may use at most 64 MiB of HBM per device.

v0:
```python
import jax
import jax.numpy as jnp
from jax import lax
from jax.sharding import PartitionSpec as P

GROUPS = 32


def passed_along(value, axis, steps):
    count = lax.axis_size(axis)
    leading, last = (max(0, -steps), min(count, count - steps))
    return lax.ppermute(value, axis, [(source, source + steps) for source in range(leading, last)])


def with_halo(cells, sides, width):
    for axis, dim in sides:
        count = lax.axis_size(axis)
        ends = count - 1
        head = lax.slice_in_dim(cells, 0, width, axis=dim)
        tail = lax.slice_in_dim(cells, cells.shape[dim] - width, cells.shape[dim], axis=dim)
        cells = jnp.concatenate(
            [
                lax.ppermute(tail, axis, [(i, (i + 1) % count) for i in range(ends)]),
                cells,
                lax.ppermute(head, axis, [((i + 1) % count, i) for i in range(ends)]),
            ],
            axis=dim,
        )
    return cells


def group_stats(values, total_cells):
    channels = values.shape[-1]
    grouped = values.reshape(-1, GROUPS, channels // GROUPS)
    cell_count = total_cells * (channels // GROUPS)
    group_mean = lax.psum(jnp.sum(grouped, axis=(0, 2)), ("section", "tm", "tile")) / cell_count
    centered = grouped - group_mean[None, :, None]
    spread = (
        lax.psum(jnp.sum(centered * centered, axis=(0, 2)), ("section", "tm", "tile")) / cell_count
    )
    inv_scale = lax.rsqrt(spread + 1e-06)
    return (jnp.repeat(group_mean, channels // GROUPS), jnp.repeat(inv_scale, channels // GROUPS))


def normalize(values, group_mean, inv_scale, norm_gain, norm_shift):
    normed = (values.astype(jnp.float32) - group_mean) * inv_scale * norm_gain + norm_shift
    return jax.nn.silu(normed).astype(jnp.bfloat16)


def pad_block(local_block):
    previous = passed_along(local_block, "tm", 1)
    first_frame = jnp.broadcast_to(local_block[:1], previous.shape)
    previous = jnp.where(lax.axis_index("tm") == 0, first_frame, previous)
    extended = jnp.concatenate([previous, local_block], axis=0)
    padded = with_halo(extended, (("section", 2), ("tile", 1)), 1)
    upper_rim = jnp.where(lax.axis_index("tile") == 0, padded[:, 1:2], padded[:, :1])
    bottom = jnp.where(
        lax.axis_index("tile") == lax.axis_size("tile") - 1, padded[:, -2:-1], padded[:, -1:]
    )
    padded = jnp.concatenate([upper_rim, padded[:, 1:-1], bottom], axis=1)
    left_rim = jnp.where(lax.axis_index("section") == 0, padded[:, :, 1:2], padded[:, :, :1])
    right_rim = jnp.where(
        lax.axis_index("section") == lax.axis_size("section") - 1,
        padded[:, :, -2:-1],
        padded[:, :, -1:],
    )
    return jnp.concatenate([left_rim, padded[:, :, 1:-1], right_rim], axis=2)


def prepare(local_block, total_cells, norm_gain, norm_shift):
    group_mean, inv_scale = group_stats(local_block.astype(jnp.float32), total_cells)
    return pad_block(normalize(local_block, group_mean, inv_scale, norm_gain, norm_shift))


def convolve(padded, weights, conv_bias):
    frames = padded.shape[0] - 2
    row_count = padded.shape[1] - 2
    columns = padded.shape[2] - 2
    channels = weights.shape[3]
    outputs = weights.shape[4]
    summed = jnp.zeros((frames, row_count, columns, outputs), jnp.float32)
    for tap_t in range(3):
        for tap_h in range(3):
            time_slab = padded[tap_t : tap_t + frames, tap_h : tap_h + row_count]
            window = jnp.concatenate(
                [time_slab[:, :, tap_w : tap_w + columns] for tap_w in range(3)], axis=-1
            )
            kernel = weights[tap_t, tap_h].reshape(3 * channels, outputs)
            summed = summed + jnp.einsum(
                "frck,ko->frco", window, kernel, preferred_element_type=jnp.float32
            )
    return summed + conv_bias


def shards(
    features,
    norm_gain_in,
    norm_shift_in,
    conv_in_weight,
    conv_in_bias,
    norm_gain_mid,
    norm_shift_mid,
    conv_mid_weight,
    conv_mid_bias,
    skip_weight,
    skip_bias,
):
    local_block = lax.all_to_all(features, "section", split_axis=2, concat_axis=3, tiled=True)
    frames, row_count, columns, channels = local_block.shape
    total_cells = (
        frames
        * row_count
        * columns
        * lax.axis_size("section")
        * lax.axis_size("tm")
        * lax.axis_size("tile")
    )
    act_in = prepare(local_block, total_cells, norm_gain_in, norm_shift_in)
    hidden = convolve(act_in, conv_in_weight, conv_in_bias).astype(jnp.bfloat16)
    act_mid = prepare(hidden, total_cells, norm_gain_mid, norm_shift_mid)
    residual = convolve(act_mid, conv_mid_weight, conv_mid_bias)
    shortcut = (
        jnp.einsum("frck,ko->frco", local_block, skip_weight, preferred_element_type=jnp.float32)
        + skip_bias
    )
    return (residual + shortcut).astype(jnp.bfloat16)


def solution(mesh):
    in_specs = (P("tm", "tile", None, "section"), P(), P(), P(), P(), P(), P(), P(), P(), P(), P())
    out_specs = P("tm", "tile", "section", None)
    return jax.shard_map(shards, mesh=mesh, in_specs=in_specs, out_specs=out_specs, check_vma=False)
```

profile of v0, /device:TPU:0, one launch (start us, length us, event | category | flops | bytes accessed | tf_op | source)
XLA Modules:
  0.0 233.7 jit_solution(4829206725132027764)
XLA Ops:
  0.0 1.2 copy.14
  1.2 3.9 %all_to_all.18 = bf16[2,8,64,128]{3,1,0,2:T(8,128)(2,1)S(1)} all-to-all(bf16[2,8,64,128]{3,1,0,2:T(8,128)(2,1)S(1)} %copy.14), channel_id=1, replica_groups=mesh['section'=2,'tm'=8,'tile'=2] {'section'}, dimensions={2} | all-to-all | bytes 524288 | tf_op jit(solution)/shard_map/all_to_all | solution.py:108
  5.1 0.5 convert_reduce_fusion
  5.9 42.0 %psum.28 = f32[32]{0:T(128)S(1)} all-reduce(f32[32]{0:T(128)S(1)} %reduce_sum.51), channel_id=1, replica_groups=mesh['section'=2,'tm'=8,'tile'=2] {'section','tm','tile'}, use_global_device_ids=true, to_apply=%region_2.0 | all-reduce | flops 32 | bytes 256 | tf_op jit(solution)/shard_map/psum | solution.py:36
  48.1 0.6 fusion.56
  49.2 40.2 %psum.29 = f32[32]{0:T(128)S(1)} all-reduce(f32[32]{0:T(128)S(1)} %reduce_sum.54), channel_id=1, replica_groups=mesh['section'=2,'tm'=8,'tile'=2] {'section','tm','tile'}, use_global_device_ids=true, to_apply=%region_5.6 | all-reduce | flops 32 | bytes 256 | tf_op jit(solution)/shard_map/psum | solution.py:39
  90.1 4.3 %collective-permute-start = (bf16[2,8,32,256]{3,2,1,0:T(8,128)(2,1)S(1)}, bf16[2,8,32,256]{3,2,1,0:T(8,128)(2,1)S(1)}, u32[]{:S(2)}, u32[]{:S(2)}) collective-permute-start(bf16[2,8,32,256]{3,2,1,0:T(8,128)(2,1)S(1)} %multiply_convert_fusion), channel_id=1, source_target_pairs={{0,2},{2,4},{4,6},{6,8},{8,10},{10,12},{12,14},{1,3},{3,5},{5,7},{... | collective-permute-start | bytes 786440 | tf_op jit(solution)/shard_map/ppermute | solution.py:12
  94.5 4.6 %collective-permute-done = bf16[2,8,32,256]{3,2,1,0:T(8,128)(2,1)S(1)} collective-permute-done((bf16[2,8,32,256]{3,2,1,0:T(8,128)(2,1)S(1)}, bf16[2,8,32,256]{3,2,1,0:T(8,128)(2,1)S(1)}, u32[]{:S(2)}, u32[]{:S(2)}) %collective-permute-start) | collective-permute-done | bytes 262176 | tf_op jit(solution)/shard_map/ppermute | solution.py:12
  99.2 1.3 collective-permute-start.1
  100.5 1.3 collective-permute-start.2
  101.8 1.8 collective-permute-done.2
  103.6 2.6 %collective-permute-start.3 = (bf16[4,1,34,256]{3,2,1,0:T(8,128)(2,1)S(1)}, bf16[4,1,34,256]{3,2,1,0:T(8,128)(2,1)S(1)}, u32[]{:S(2)}, u32[]{:S(2)}) collective-permute-start(bf16[4,1,34,256]{3,2,1,0:T(8,128)(2,1)S(1)} %pad_maximum_fusion.10), channel_id=1, source_target_pairs={{0,1},{2,3},{4,5},{6,7},{8,9},{10,11},{12,13},{14,15},{16,17},{18,... | collective-permute-start | bytes 208904 | tf_op jit(solution)/shard_map/ppermute | solution.py:23
  106.2 2.0 collective-permute-done.3
  108.2 0.7 broadcast_select_fusion.4
  108.9 1.3 collective-permute-start.4
  110.2 1.1 fusion.157
  111.2 4.2 %collective-permute-done.4 = bf16[4,1,34,256]{3,2,1,0:T(8,128)(2,1)S(1)} collective-permute-done((bf16[4,1,34,256]{3,2,1,0:T(8,128)(2,1)}, bf16[4,1,34,256]{3,2,1,0:T(8,128)(2,1)S(1)}, u32[]{:S(2)}, u32[]{:S(2)}) %collective-permute-start.4) | collective-permute-done | bytes 69664 | tf_op jit(solution)/shard_map/ppermute | solution.py:25
  115.4 0.4 pad_maximum_fusion
  115.8 0.3 slice.529
  116.3 0.5 fusion.114
  116.9 0.6 fusion.106
  117.5 0.5 pad_maximum_fusion.4
  118.0 0.5 fusion.159
  118.5 0.4 copy-done.8
  118.9 0.4 fusion.16
  119.5 0.4 convolution_add_fusion.16
  119.9 0.4 copy-done.6
  120.2 0.4 convolution_add_fusion.15
  120.8 0.4 convolution_add_fusion.14
  121.2 0.4 copy-done.4
  121.5 0.4 convolution_add_fusion.13
  121.9 0.6 copy-done.3
  122.5 0.4 convolution_add_fusion.12
  122.8 0.4 convolution_add_fusion.11
  123.2 0.4 convolution_add_fusion.10
  123.9 0.4 fusion.163
  124.5 41.1 %psum.30 = f32[32]{0:T(128)S(1)} all-reduce(f32[32]{0:T(128)S(1)} %reduce_sum.72), channel_id=1, replica_groups=mesh['section'=2,'tm'=8,'tile'=2] {'section','tm','tile'}, use_global_device_ids=true, to_apply=%region_8.9 | all-reduce | flops 32 | bytes 256 | tf_op jit(solution)/shard_map/psum | solution.py:36
  166.1 39.6 %psum.31 = f32[32]{0:T(128)S(1)} all-reduce(f32[32]{0:T(128)S(1)} %reduce_sum.75), channel_id=1, replica_groups=mesh['section'=2,'tm'=8,'tile'=2] {'section','tm','tile'}, use_global_device_ids=true, to_apply=%region_11.12 | all-reduce | flops 32 | bytes 256 | tf_op jit(solution)/shard_map/psum | solution.py:39
  206.0 4.2 %collective-permute-start.5 = (bf16[2,8,32,128]{3,2,1,0:T(8,128)(2,1)S(1)}, bf16[2,8,32,128]{3,2,1,0:T(8,128)(2,1)S(1)}, u32[]{:S(2)}, u32[]{:S(2)}) collective-permute-start(bf16[2,8,32,128]{3,2,1,0:T(8,128)(2,1)S(1)} %multiply_convert_fusion.1), channel_id=1, source_target_pairs={{0,2},{2,4},{4,6},{6,8},{8,10},{10,12},{12,14},{1,3},{3,5},{5,7},{... | collective-permute-start | bytes 393224 | tf_op jit(solution)/shard_map/ppermute | solution.py:12
  210.2 2.5 %collective-permute-done.5 = bf16[2,8,32,128]{3,2,1,0:T(8,128)(2,1)S(1)} collective-permute-done((bf16[2,8,32,128]{3,2,1,0:T(8,128)(2,1)S(1)}, bf16[2,8,32,128]{3,2,1,0:T(8,128)(2,1)S(1)}, u32[]{:S(2)}, u32[]{:S(2)}) %collective-permute-start.5) | collective-permute-done | bytes 131104 | tf_op jit(solution)/shard_map/ppermute | solution.py:12
  212.7 1.5 collective-permute-start.6
  214.2 1.3 collective-permute-start.7
  215.5 1.8 collective-permute-done.7
  217.3 3.9 %collective-permute-start.8 = (bf16[4,1,34,128]{3,2,1,0:T(8,128)(2,1)S(1)}, bf16[4,1,34,128]{3,2,1,0:T(8,128)(2,1)S(1)}, u32[]{:S(2)}, u32[]{:S(2)}) collective-permute-start(bf16[4,1,34,128]{3,2,1,0:T(8,128)(2,1)S(1)} %pad_maximum_fusion.14), channel_id=1, source_target_pairs={{0,1},{2,3},{4,5},{6,7},{8,9},{10,11},{12,13},{14,15},{16,17},{18,... | collective-permute-start | bytes 104456 | tf_op jit(solution)/shard_map/ppermute | solution.py:23
  221.2 1.7 collective-permute-done.8
  222.9 1.3 collective-permute-start.9
  224.3 4.5 %collective-permute-done.9 = bf16[4,1,34,128]{3,2,1,0:T(8,128)(2,1)S(1)} collective-permute-done((bf16[4,1,34,128]{3,2,1,0:T(8,128)(2,1)S(1)}, bf16[4,1,34,128]{3,2,1,0:T(8,128)(2,1)S(1)}, u32[]{:S(2)}, u32[]{:S(2)}) %collective-permute-start.9) | collective-permute-done | bytes 34848 | tf_op jit(solution)/shard_map/ppermute | solution.py:25
  232.8 0.9 fusion.3
  (90 shorter events, 7.6 us)
Async XLA Ops:
  0.0 232.7 %copy-start = (bf16[256,128]{1,0:T(8,128)(2,1)S(1)}, bf16[256,128]{1,0:T(8,128)(2,1)}, u32[]{:S(2)}) copy-start(bf16[256,128]{1,0:T(8,128)(2,1)} %param.20) | copy-start | bytes 196612
  0.0 89.9 %copy-start.10 = (f32[256]{0:T(256)S(1)}, f32[256]{0:T(256)}, u32[]{:S(2)}) copy-start(f32[256]{0:T(256)} %param.12) | copy-start | bytes 3076
  0.0 89.9 %copy-start.9 = (f32[256]{0:T(256)S(1)}, f32[256]{0:T(256)}, u32[]{:S(2)}) copy-start(f32[256]{0:T(256)} %param.13) | copy-start | bytes 3076
  90.1 20.1 %copy-start.1 = (bf16[3,3,3,256,128]{4,3,2,1,0:T(8,128)(2,1)S(1)}, bf16[3,3,3,256,128]{4,3,2,1,0:T(8,128)(2,1)}, u32[]{:S(2)}) copy-start(bf16[3,3,3,256,128]{4,3,2,1,0:T(8,128)(2,1)} %param.14) | copy-start | bytes 5308420
  90.1 9.0 %collective-permute-start = (bf16[2,8,32,256]{3,2,1,0:T(8,128)(2,1)S(1)}, bf16[2,8,32,256]{3,2,1,0:T(8,128)(2,1)S(1)}, u32[]{:S(2)}, u32[]{:S(2)}) collective-permute-start(bf16[2,8,32,256]{3,2,1,0:T(8,128)(2,1)S(1)} %multiply_convert_fusion), channel_id=1, source_target_pairs={{0,2},{2,4},{4,6},{6,8},{8,10},{10,12},{12,14},{1,3},{3,5},{5,7},{... | collective-permute-start | bytes 786440 | tf_op jit(solution)/shard_map/ppermute | solution.py:12
  99.2 2.6 %collective-permute-start.1 = (bf16[4,8,1,256]{3,2,1,0:T(2,128)(2,1)S(1)}, bf16[4,8,1,256]{3,2,1,0:T(2,128)(2,1)S(1)}, u32[]{:S(2)}, u32[]{:S(2)}) collective-permute-start(bf16[4,8,1,256]{3,2,1,0:T(2,128)(2,1)S(1)} %get-tuple-element.51), channel_id=1, source_target_pairs={{0,16},{1,17},{2,18},{3,19},{4,20},{5,21},{6,22},{7,23},{8,24},{9,... | collective-permute-start | bytes 49160 | tf_op jit(solution)/shard_map/ppermute | solution.py:23
  100.5 3.1 %collective-permute-start.2 = (bf16[4,8,1,256]{3,2,1,0:T(2,128)(2,1)S(1)}, bf16[4,8,1,256]{3,2,1,0:T(2,128)(2,1)S(1)}, u32[]{:S(2)}, u32[]{:S(2)}) collective-permute-start(bf16[4,8,1,256]{3,2,1,0:T(2,128)(2,1)S(1)} %get-tuple-element.52), channel_id=1, source_target_pairs={{16,0},{17,1},{18,2},{19,3},{20,4},{21,5},{22,6},{23,7},{24,8},{25... | collective-permute-start | bytes 49160 | tf_op jit(solution)/shard_map/ppermute | solution.py:25
  103.6 4.6 %collective-permute-start.3 = (bf16[4,1,34,256]{3,2,1,0:T(8,128)(2,1)S(1)}, bf16[4,1,34,256]{3,2,1,0:T(8,128)(2,1)S(1)}, u32[]{:S(2)}, u32[]{:S(2)}) collective-permute-start(bf16[4,1,34,256]{3,2,1,0:T(8,128)(2,1)S(1)} %pad_maximum_fusion.10), channel_id=1, source_target_pairs={{0,1},{2,3},{4,5},{6,7},{8,9},{10,11},{12,13},{14,15},{16,17},{18,... | collective-permute-start | bytes 208904 | tf_op jit(solution)/shard_map/ppermute | solution.py:23
  108.9 6.5 %collective-permute-start.4 = (bf16[4,1,34,256]{3,2,1,0:T(8,128)(2,1)}, bf16[4,1,34,256]{3,2,1,0:T(8,128)(2,1)S(1)}, u32[]{:S(2)}, u32[]{:S(2)}) collective-permute-start(bf16[4,1,34,256]{3,2,1,0:T(8,128)(2,1)} %get-tuple-element.8), channel_id=1, source_target_pairs={{1,0},{3,2},{5,4},{7,6},{9,8},{11,10},{13,12},{15,14},{17,16},{19,... | collective-permute-start | bytes 208904 | tf_op jit(solution)/shard_map/ppermute | solution.py:25
  118.0 0.9 copy-start.8
  118.5 1.0 copy-start.7
  119.3 1.0 copy-start.6
  119.8 1.0 copy-start.5
  120.6 1.0 copy-start.4
  121.5 0.9 copy-start.3
  123.2 0.7 copy-start.14
  123.9 82.0 %copy-start.11 = (f32[128]{0:T(128)S(1)}, f32[128]{0:T(128)}, u32[]{:S(2)}) copy-start(f32[128]{0:T(128)} %param.17) | copy-start | bytes 1540
  123.9 82.0 %copy-start.12 = (f32[128]{0:T(128)S(1)}, f32[128]{0:T(128)}, u32[]{:S(2)}) copy-start(f32[128]{0:T(128)} %param.16) | copy-start | bytes 1540
  124.3 99.9 %copy-start.2 = (bf16[3,3,3,128,128]{4,3,2,1,0:T(8,128)(2,1)S(1)}, bf16[3,3,3,128,128]{4,3,2,1,0:T(8,128)(2,1)}, u32[]{:S(2)}) copy-start(bf16[3,3,3,128,128]{4,3,2,1,0:T(8,128)(2,1)} %param.18) | copy-start | bytes 2654212
  206.0 6.7 %collective-permute-start.5 = (bf16[2,8,32,128]{3,2,1,0:T(8,128)(2,1)S(1)}, bf16[2,8,32,128]{3,2,1,0:T(8,128)(2,1)S(1)}, u32[]{:S(2)}, u32[]{:S(2)}) collective-permute-start(bf16[2,8,32,128]{3,2,1,0:T(8,128)(2,1)S(1)} %multiply_convert_fusion.1), channel_id=1, source_target_pairs={{0,2},{2,4},{4,6},{6,8},{8,10},{10,12},{12,14},{1,3},{3,5},{5,7},{... | collective-permute-start | bytes 393224 | tf_op jit(solution)/shard_map/ppermute | solution.py:12
  212.7 2.8 %collective-permute-start.6 = (bf16[4,8,1,128]{3,2,1,0:T(2,128)(2,1)S(1)}, bf16[4,8,1,128]{3,2,1,0:T(2,128)(2,1)S(1)}, u32[]{:S(2)}, u32[]{:S(2)}) collective-permute-start(bf16[4,8,1,128]{3,2,1,0:T(2,128)(2,1)S(1)} %get-tuple-element.77), channel_id=1, source_target_pairs={{0,16},{1,17},{2,18},{3,19},{4,20},{5,21},{6,22},{7,23},{8,24},{9,... | collective-permute-start | bytes 24584 | tf_op jit(solution)/shard_map/ppermute | solution.py:23
  214.2 3.1 %collective-permute-start.7 = (bf16[4,8,1,128]{3,2,1,0:T(2,128)(2,1)S(1)}, bf16[4,8,1,128]{3,2,1,0:T(2,128)(2,1)S(1)}, u32[]{:S(2)}, u32[]{:S(2)}) collective-permute-start(bf16[4,8,1,128]{3,2,1,0:T(2,128)(2,1)S(1)} %get-tuple-element.78), channel_id=1, source_target_pairs={{16,0},{17,1},{18,2},{19,3},{20,4},{21,5},{22,6},{23,7},{24,8},{25... | collective-permute-start | bytes 24584 | tf_op jit(solution)/shard_map/ppermute | solution.py:25
  217.3 5.5 %collective-permute-start.8 = (bf16[4,1,34,128]{3,2,1,0:T(8,128)(2,1)S(1)}, bf16[4,1,34,128]{3,2,1,0:T(8,128)(2,1)S(1)}, u32[]{:S(2)}, u32[]{:S(2)}) collective-permute-start(bf16[4,1,34,128]{3,2,1,0:T(8,128)(2,1)S(1)} %pad_maximum_fusion.14), channel_id=1, source_target_pairs={{0,1},{2,3},{4,5},{6,7},{8,9},{10,11},{12,13},{14,15},{16,17},{18,... | collective-permute-start | bytes 104456 | tf_op jit(solution)/shard_map/ppermute | solution.py:23
  222.9 5.9 %collective-permute-start.9 = (bf16[4,1,34,128]{3,2,1,0:T(8,128)(2,1)S(1)}, bf16[4,1,34,128]{3,2,1,0:T(8,128)(2,1)S(1)}, u32[]{:S(2)}, u32[]{:S(2)}) collective-permute-start(bf16[4,1,34,128]{3,2,1,0:T(8,128)(2,1)S(1)} %get-tuple-element.6), channel_id=1, source_target_pairs={{1,0},{3,2},{5,4},{7,6},{9,8},{11,10},{13,12},{15,14},{17,16},{19,... | collective-permute-start | bytes 104456 | tf_op jit(solution)/shard_map/ppermute | solution.py:25
  231.8 0.7 copy-start.15
  232.1 0.7 copy-start.13
where the time goes:
time: 235 us; the launch traced here: 234 us
  blocking collectives  167 us (71%)
  waiting for transfers between devices  23 us (10%)
  starting transfers between devices  22.9 us (10%)
  local copies, waits for them, and re-layouts  7.64 us (3%)
  matrix products  6.65 us (3%)
  other arithmetic  6.07 us (3%)
    psum x2, blocking collectives, group_stats(): lax.psum(jnp.sum(grouped, axis=(0, 2)), ('section', 'tm', 'tile'))  83.1 us
    psum x2, blocking collectives, group_stats(): lax.psum(jnp.sum(centered * centered, axis=(0, 2)), ('section', 'tm', 'ti...  79.7 us
    ppermute x4, waiting for transfers between devices, with_halo(): lax.ppermute(head, axis, [((i + 1) % count, i) for i in range(ends)])  12.2 us
    ppermute x4, starting transfers between devices, with_halo(): lax.ppermute(tail, axis, [(i, (i + 1) % count) for i in range(ends)])  9.2 us
    ppermute x2, starting transfers between devices, passed_along(): lax.ppermute(value, axis, [(source, source + steps) for source in range(l...  8.51 us
    ppermute x2, waiting for transfers between devices, passed_along(): lax.ppermute(value, axis, [(source, source + steps) for source in range(l...  7.1 us
    dot_general x18, matrix products, convolve(): jnp.einsum('frck,ko->frco', window, kernel, preferred_element_type=jnp.fl...  5.76 us
    ppermute x4, starting transfers between devices, with_halo(): lax.ppermute(head, axis, [((i + 1) % count, i) for i in range(ends)])  5.16 us
  transfers between devices with their start and end apart: 10, of which 8 were waited for; matrix products, arithmetic and copies ran while one was open for 0% of the time, Pallas kernels for 0%

commit v1 on v0

v1 whole, which is shorter than its diff:
```python
import jax
import jax.numpy as jnp
from jax import lax
from jax.sharding import PartitionSpec as P

GROUPS = 32
AXES = ("section", "tm", "tile")


def local_moments(values):
    cells = values.astype(jnp.float32)
    mean = jnp.mean(cells, axis=(0, 1, 2))
    centered = cells - mean
    return jnp.stack([mean, jnp.sum(centered * centered, axis=(0, 1, 2))])


def combine(moments, cells, group_width):
    devices, _, channels = moments.shape
    groups = channels // group_width
    means = moments[:, 0].reshape(devices, groups, group_width)
    spreads = moments[:, 1].reshape(devices, groups, group_width)
    group_mean = jnp.mean(means, axis=(0, 2))
    off = means - group_mean[None, :, None]
    spread = jnp.sum(spreads + cells * off * off, axis=(0, 2)) / (cells * devices * group_width)
    inv = lax.rsqrt(spread + 1e-6)
    return jnp.repeat(group_mean, group_width), jnp.repeat(inv, group_width)


def normalize(values, mean, inv, gain, shift):
    normed = (values.astype(jnp.float32) - mean) * inv * gain + shift
    return jax.nn.silu(normed).astype(jnp.bfloat16)


def convolve(padded, weights):
    frames, rows, columns = (padded.shape[0] - 2, padded.shape[1] - 2, padded.shape[2] - 2)
    channels, outputs = weights.shape[3:]
    summed = jnp.zeros((frames, rows, columns, outputs), jnp.float32)
    for t in range(3):
        for h in range(3):
            slab = padded[t : t + frames, h : h + rows]
            window = jnp.concatenate([slab[:, :, w : w + columns] for w in range(3)], axis=-1)
            summed = summed + jnp.einsum(
                "frck,ko->frco",
                window,
                weights[t, h].reshape(3 * channels, outputs),
                preferred_element_type=jnp.float32,
            )
    return summed


def pairs_for(tm_count, tile_count, tm_step, tile_step):
    out = []
    for a in range(tm_count):
        for b in range(tile_count):
            c, d = a + tm_step, b + tile_step
            if 0 <= c < tm_count and 0 <= d < tile_count:
                out.append((a * tile_count + b, c * tile_count + d))
    return out


def shards(
    features,
    norm_gain_in,
    norm_shift_in,
    conv_in_weight,
    conv_in_bias,
    norm_gain_mid,
    norm_shift_mid,
    conv_mid_weight,
    conv_mid_bias,
    skip_weight,
    skip_bias,
):
    sections, tms, tiles = (lax.axis_size(axis) for axis in AXES)
    devices = sections * tms * tiles
    section, tm, tile = (lax.axis_index(axis) for axis in AXES)
    frames, rows, columns, half = features.shape
    own = columns // sections
    group_in = half * sections // GROUPS

    previous = lax.ppermute(features, ("tm", "tile"), pairs_for(tms, tiles, 1, 0))
    top, bottom = features[:, :2], features[:, -2:]
    up = lax.ppermute(bottom, ("tm", "tile"), pairs_for(tms, tiles, 0, 1))
    down = lax.ppermute(top, ("tm", "tile"), pairs_for(tms, tiles, 0, -1))
    up_prev = lax.ppermute(bottom, ("tm", "tile"), pairs_for(tms, tiles, 1, 1))
    down_prev = lax.ppermute(top, ("tm", "tile"), pairs_for(tms, tiles, 1, -1))

    gathered = lax.all_gather(local_moments(features), AXES)
    gathered = gathered.reshape(sections, tms * tiles, 2, half)
    gathered = jnp.concatenate([gathered[s] for s in range(sections)], axis=-1)
    mean_in, inv_in = combine(gathered, frames * rows * columns, group_in)

    now = jnp.concatenate([up, features, down], axis=1)
    before = jnp.concatenate([up_prev, previous, down_prev], axis=1)
    block = jnp.concatenate([jnp.where(tm == 0, now[:1], before), now], axis=0)
    row_ids = jnp.arange(rows + 4)[None, :, None, None]
    block = jnp.where((tile == 0) & (row_ids < 2), block[:, 2:3], block)
    block = jnp.where((tile == tiles - 1) & (row_ids >= rows + 2), block[:, -3:-2], block)
    left = block[:, :, : own + 2]
    right = block[:, :, own - 2 :]
    got = lax.ppermute(
        jnp.where(section == 0, right, left), "section", [(0, 1), (1, 0)]
    )
    kept = jnp.where(section == 0, left, right)
    whole = jnp.where(
        section == 0,
        jnp.concatenate([kept, got], axis=-1),
        jnp.concatenate([got, kept], axis=-1),
    )
    at_left = jnp.concatenate([whole[:, :, :1], whole[:, :, :1], whole], axis=2)
    at_right = jnp.concatenate([whole, whole[:, :, -1:], whole[:, :, -1:]], axis=2)
    whole = jnp.where(section == 0, at_left, at_right)

    act_in = normalize(whole, mean_in, inv_in, norm_gain_in, norm_shift_in)
    hidden = (convolve(act_in, conv_in_weight) + conv_in_bias).astype(jnp.bfloat16)
    row_ids = jnp.arange(rows + 2)[None, :, None, None]
    col_ids = jnp.arange(own + 2)[None, None, :, None]
    hidden = jnp.where((tile == 0) & (row_ids == 0), hidden[:, 1:2], hidden)
    hidden = jnp.where((tile == tiles - 1) & (row_ids == rows + 1), hidden[:, -2:-1], hidden)
    hidden = jnp.where((section == 0) & (col_ids == 0), hidden[:, :, 1:2], hidden)
    hidden = jnp.where(
        (section == sections - 1) & (col_ids == own + 1), hidden[:, :, -2:-1], hidden
    )
    before = lax.ppermute(hidden, "tm", [(i, i + 1) for i in range(tms - 1)])
    moments = local_moments(hidden[:, 1:-1, 1:-1])
    moments = lax.all_to_all(
        jnp.broadcast_to(moments, (devices, *moments.shape)), AXES, 0, 0, tiled=True
    )
    mean_mid, inv_mid = combine(moments, frames * rows * own, hidden.shape[-1] // GROUPS)
    block = jnp.concatenate([jnp.where(tm == 0, hidden[:1], before), hidden], axis=0)
    act_mid = normalize(block, mean_mid, inv_mid, norm_gain_mid, norm_shift_mid)
    residual = convolve(act_mid, conv_mid_weight) + conv_mid_bias
    shortcut = jnp.einsum(
        "frck,ko->frco",
        whole[frames:, 2:-2, 2:-2],
        skip_weight,
        preferred_element_type=jnp.float32,
    )
    return (residual + (shortcut + skip_bias)).astype(jnp.bfloat16)


def solution(mesh):
    in_specs = (P("tm", "tile", None, "section"),) + (P(),) * 10
    out_specs = P("tm", "tile", "section", None)
    return jax.shard_map(shards, mesh=mesh, in_specs=in_specs, out_specs=out_specs, check_vma=False)
```

time: 235 us -> 114 us (0.49)
  blocking collectives: 167 us -> 63.7 us
  waiting for transfers between devices: 23 us -> 4.17 us
    psum x4 -> x0, blocking collectives: 163 us -> none  [the longest x2 83.1 us: group_stats(): lax.psum(jnp.sum(grouped, axis=(0, 2)), ('section', 'tm', 'tile'))]
    all_gather x0 -> x1, blocking collectives: none -> 63.7 us  [shards(): gathered = lax.all_gather(local_moments(features), AXES)]
    ppermute x10 -> x7, waiting for transfers between devices: 23 us -> 0.85 us  [the longest x1 0.6 us: shards(): lax.ppermute(jnp.where(section == 0, right, left), 'section', [(0, 1), (1...]
    all_to_all x1 -> x0, blocking collectives: 3.94 us -> none  [shards(): lax.all_to_all(features, 'section', split_axis=2, concat_axis=3, tiled=True)]
    ppermute x10 -> x7, starting transfers between devices: 22.9 us -> 19.1 us  [the longest x1 8.54 us: shards(): up_prev = lax.ppermute(bottom, ('tm', 'tile'), pairs_for(tms, tiles, 1, 1))]
    all_to_all x0 -> x1, waiting for transfers between devices: none -> 3.32 us  [shards(): lax.all_to_all(jnp.broadcast_to(moments, (devices, *moments.shape)), AXES...]
    concatenate x10 -> x0, other arithmetic: 2.91 us -> none  [the longest x4 1.57 us: pad_block(): return jnp.concatenate([left_rim, padded[:, :, 1:-1], right_rim], axis=2)]
    slice x7 -> x14, local copies, waits for them, and re-layouts: 2.28 us -> 4.94 us  [the longest x4 2.86 us: convolve(): slab[:, :, w:w + columns]]
  transfers between devices with their start and end apart: 10 -> 8, of which waited for: 8 -> 3; matrix products, arithmetic and copies ran while one was open for 0% -> 4% of each run, Pallas kernels for 0% -> 0%
where the time goes in v1:
time: 114 us; the launch traced here: 113 us
  blocking collectives  63.7 us (56%)
  starting transfers between devices  21.7 us (19%)
  local copies, waits for them, and re-layouts  8.42 us (7%)
  matrix products  7.95 us (7%)
  other arithmetic  6 us (5%)
  waiting for transfers between devices  4.17 us (4%)
    all_gather x1, blocking collectives, shards(): gathered = lax.all_gather(local_moments(features), AXES)  63.7 us
    ppermute x1, starting transfers between devices, shards(): up_prev = lax.ppermute(bottom, ('tm', 'tile'), pairs_for(tms, tiles, 1, 1))  8.54 us
    dot_general x18, matrix products, convolve(): jnp.einsum('frck,ko->frco', window, weights[t, h].reshape(3 * channels, o...  7.05 us
    ppermute x1, starting transfers between devices, shards(): before = lax.ppermute(hidden, 'tm', [(i, i + 1) for i in range(tms - 1)])  3.86 us
    ppermute x1, starting transfers between devices, shards(): lax.ppermute(features, ('tm', 'tile'), pairs_for(tms, tiles, 1, 0))  3.41 us
    all_to_all x1, waiting for transfers between devices, shards(): lax.all_to_all(jnp.broadcast_to(moments, (devices, *moments.shape)), AXES...  3.32 us
    slice x4, local copies, waits for them, and re-layouts, convolve(): slab[:, :, w:w + columns]  2.86 us
    all_to_all x1, starting transfers between devices, shards(): lax.all_to_all(jnp.broadcast_to(moments, (devices, *moments.shape)), AXES...  2.59 us
  transfers between devices with their start and end apart: 8, of which 3 were waited for; matrix products, arithmetic and copies ran while one was open for 4% of the time, Pallas kernels for 0%

profile of v1, /device:TPU:0, one launch (start us, length us, event | category | flops | bytes accessed | tf_op | source)
XLA Modules:
  0.0 112.7 jit_solution(14373421010172854157)
XLA Ops:
  0.0 1.0 fusion.173
  1.0 0.7 collective-permute-start.4
  1.7 1.3 %collective-permute-start.1 = (bf16[2,2,64,128]{3,2,1,0:T(8,128)(2,1)S(1)}, bf16[2,2,64,128]{3,2,1,0:T(8,128)(2,1)S(1)}, u32[]{:S(2)}, u32[]{:S(2)}) collective-permute-start(bf16[2,2,64,128]{3,2,1,0:T(8,128)(2,1)S(1)} %get-tuple-element.83), channel_id=1, source_target_pairs={{1,0},{3,2},{5,4},{7,6},{9,8},{11,10},{13,12},{15,14},{17,16},{19,... | collective-permute-start | bytes 196616 | tf_op jit(solution)/shard_map/ppermute | solution.py:84
  3.0 8.5 %collective-permute-start.2 = (bf16[2,2,64,128]{3,2,1,0:T(8,128)(2,1)S(1)}, bf16[2,2,64,128]{3,2,1,0:T(8,128)(2,1)S(1)}, u32[]{:S(2)}, u32[]{:S(2)}) collective-permute-start(bf16[2,2,64,128]{3,2,1,0:T(8,128)(2,1)S(1)} %get-tuple-element.84), channel_id=1, source_target_pairs={{0,3},{2,5},{4,7},{6,9},{8,11},{10,13},{12,15},{16,19},{18,21},{20... | collective-permute-start | bytes 196616 | tf_op jit(solution)/shard_map/ppermute | solution.py:85
  11.5 1.3 %collective-permute-start = (bf16[2,2,64,128]{3,2,1,0:T(8,128)(2,1)S(1)}, bf16[2,2,64,128]{3,2,1,0:T(8,128)(2,1)S(1)}, u32[]{:S(2)}, u32[]{:S(2)}) collective-permute-start(bf16[2,2,64,128]{3,2,1,0:T(8,128)(2,1)S(1)} %get-tuple-element.84), channel_id=1, source_target_pairs={{0,1},{2,3},{4,5},{6,7},{8,9},{10,11},{12,13},{14,15},{16,17},{18,... | collective-permute-start | bytes 196616 | tf_op jit(solution)/shard_map/ppermute | solution.py:83
  12.8 3.4 %collective-permute-start.3 = (bf16[2,8,64,128]{3,2,1,0:T(8,128)(2,1)}, bf16[2,8,64,128]{3,2,1,0:T(8,128)(2,1)S(1)}, u32[]{:S(2)}, u32[]{:S(2)}) collective-permute-start(bf16[2,8,64,128]{3,2,1,0:T(8,128)(2,1)} %param.11), channel_id=1, source_target_pairs={{0,2},{1,3},{2,4},{3,5},{4,6},{5,7},{6,8},{7,9},{8,10},{9,11},{10,... | collective-permute-start | bytes 786440 | tf_op jit(solution)/shard_map/ppermute | solution.py:81
  16.3 1.1 convert_reduce_fusion
  17.4 1.1 fusion.89
  18.5 63.7 %all-gather.1 = f32[32,2,128]{2,1,0:T(2,128)S(1)} all-gather(f32[1,2,128]{2,1,0:T(2,128)S(1)} %maximum_bitcast_fusion), channel_id=2, replica_groups=mesh['section'=2,'tm'=8,'tile'=2] {'section','tm','tile'}, dimensions={0}, use_global_device_ids=true | all-gather | bytes 33792 | tf_op jit(solution)/shard_map/all_gather | solution.py:88
  82.9 0.8 fusion.170
  84.0 0.1 fusion.87
  84.3 0.2 broadcast_select_fusion.2
  84.7 0.9 copy-done.2
  85.8 0.6 collective-permute-done.5
  86.4 0.4 maximum_select_fusion
  86.9 1.3 %multiply_convert_fusion = (bf16[4,12,36,256]{3,2,1,0:T(8,128)(2,1)S(1)}, bf16[4,12,36,256]{3,2,1,0:T(8,128)(2,1)S(1)}) fusion(f32[256]{0:T(256)S(1)} %copy-done.11, f32[256]{0:T(256)S(1)} %copy-done.12, f32[256]{0:T(256)S(1)} %mul.76, f32[256]{0:T(256)S(1)} %sub.56, bf16[4,12,1,256]{3,2,1,0:T(2,128)(2,1)S(1)} %get-tuple-element.44, ...), kind=kLoop, calls=%fused_computation | loop fusion | flops 10174464 | bytes 2658305 | tf_op jit(solution)/shard_map/convert_element_type | solution.py:31
  88.2 0.3 fusion.168
  88.5 2.0 %fusion.167 = (bf16[2,10,34,256]{3,2,1,0:T(8,128)(2,1)S(1)}, bf16[2,10,34,256]{3,2,1,0:T(8,128)(2,1)S(1)}, bf16[2,10,34,256]{3,2,1,0:T(8,128)(2,1)S(1)}, bf16[2,...) fusion(bf16[4,12,36,256]{3,2,1,0:T(8,128)(2,1)S(1)} %get-tuple-, ...), kind=kLoop, calls=%fused_computation.205 | loop fusion | bytes 13230080 | tf_op jit(solution)/shard_map/slice | solution.py:41
  90.5 0.5 fusion
  91.0 0.5 fusion.75
  91.5 0.5 fusion.72
  92.0 0.5 fusion.69
  92.6 0.5 fusion.66
  93.1 0.5 fusion.63
  93.6 0.5 fusion.60
  94.2 0.5 fusion.57
  94.7 0.1 copy-done.15
  94.8 0.5 fusion.81
  95.8 0.1 broadcast_select_fusion.6
  96.1 0.6 broadcast_in_dim.163
  96.7 2.6 %all-to-all-start = ((f32[32,2,128]{2,1,0:T(2,128)}), f32[32,2,128]{2,1,0:T(2,128)S(1)}, u32[]{:S(2)}, u32[]{:S(2)}) async-start(f32[32,2,128]{2,1,0:T(2,128)} %broadcast_in_dim.163), calls=%async_computation | async-start | bytes 65536 | tf_op jit(solution)/shard_map/all_to_all | solution.py:126
  99.4 3.9 %collective-permute-start.6 = (bf16[2,10,34,128]{3,2,1,0:T(8,128)(2,1)S(1)}, bf16[2,10,34,128]{3,2,1,0:T(8,128)(2,1)S(1)}, u32[]{:S(2)}, u32[]{:S(2)}) collective-permute-start(bf16[2,10,34,128]{3,2,1,0:T(8,128)(2,1)S(1)} %broadcast_select_fusion.6), channel_id=1, source_target_pairs={{0,2},{2,4},{4,6},{6,8},{8,10},{10,12},{12,14},{1,3},{3,5},{5,7},{... | collective-permute-start | bytes 522248 | tf_op jit(solution)/shard_map/ppermute | solution.py:124
  103.2 3.3 %all-to-all-done = f32[32,2,128]{2,1,0:T(2,128)S(1)} async-done(((f32[32,2,128]{2,1,0:T(2,128)}), f32[32,2,128]{2,1,0:T(2,128)S(1)}, u32[]{:S(2)}, u32[]{:S(2)}) %all-to-all-start) | async-done | bytes 32800 | tf_op jit(solution)/shard_map/all_to_all | solution.py:126
  107.5 0.2 collective-permute-done.6
  107.8 0.3 multiply_convert_fusion.1
  108.1 0.2 fusion.172
  108.3 0.4 fusion.171
  108.7 0.4 copy-done.10
  109.1 0.3 fusion.90
  109.4 0.3 convolution_add_fusion.8
  109.7 0.3 convolution_add_fusion.7
  110.1 0.3 convolution_add_fusion.6
  110.3 0.3 convolution_add_fusion.5
  110.6 0.3 convolution_add_fusion.4
  111.0 0.3 convolution_add_fusion.3
  111.2 0.3 convolution_add_fusion.2
  111.5 0.3 fusion.85
  111.8 0.9 fusion.86
  (102 shorter events, 3.1 us)
Async XLA Ops:
  0.0 111.8 %copy-start = (bf16[256,128]{1,0:T(8,128)(2,1)S(1)}, bf16[256,128]{1,0:T(8,128)(2,1)}, u32[]{:S(2)}) copy-start(bf16[256,128]{1,0:T(8,128)(2,1)} %param.20) | copy-start | bytes 196612
  0.0 83.7 %copy-start.1 = (bf16[2,8,64,128]{3,2,1,0:T(8,128)(2,1)S(1)}, bf16[2,8,64,128]{3,2,1,0:T(8,128)(2,1)}, u32[]{:S(2)}) copy-start(bf16[2,8,64,128]{3,2,1,0:T(8,128)(2,1)} %param.11) | copy-start | bytes 786436
  0.0 82.9 %copy-start.3 = (bf16[3,3,3,128,128]{4,3,2,1,0:T(8,128)(2,1)S(1)}, bf16[3,3,3,128,128]{4,3,2,1,0:T(8,128)(2,1)}, u32[]{:S(2)}) copy-start(bf16[3,3,3,128,128]{4,3,2,1,0:T(8,128)(2,1)} %param.18) | copy-start | bytes 2654212
  1.0 82.9 %collective-permute-start.4 = (bf16[2,2,64,128]{3,2,1,0:T(8,128)(2,1)S(1)}, bf16[2,2,64,128]{3,2,1,0:T(8,128)(2,1)S(1)}, u32[]{:S(2)}, u32[]{:S(2)}) collective-permute-start(bf16[2,2,64,128]{3,2,1,0:T(8,128)(2,1)S(1)} %get-tuple-element.83), channel_id=1, source_target_pairs={{1,2},{3,4},{5,6},{7,8},{9,10},{11,12},{13,14},{17,18},{19,20},{21... | collective-permute-start | bytes 196616 | tf_op jit(solution)/shard_map/ppermute | solution.py:86
  1.7 82.1 %collective-permute-start.1 = (bf16[2,2,64,128]{3,2,1,0:T(8,128)(2,1)S(1)}, bf16[2,2,64,128]{3,2,1,0:T(8,128)(2,1)S(1)}, u32[]{:S(2)}, u32[]{:S(2)}) collective-permute-start(bf16[2,2,64,128]{3,2,1,0:T(8,128)(2,1)S(1)} %get-tuple-element.83), channel_id=1, source_target_pairs={{1,0},{3,2},{5,4},{7,6},{9,8},{11,10},{13,12},{15,14},{17,16},{19,... | collective-permute-start | bytes 196616 | tf_op jit(solution)/shard_map/ppermute | solution.py:84
  3.0 80.9 %collective-permute-start.2 = (bf16[2,2,64,128]{3,2,1,0:T(8,128)(2,1)S(1)}, bf16[2,2,64,128]{3,2,1,0:T(8,128)(2,1)S(1)}, u32[]{:S(2)}, u32[]{:S(2)}) collective-permute-start(bf16[2,2,64,128]{3,2,1,0:T(8,128)(2,1)S(1)} %get-tuple-element.84), channel_id=1, source_target_pairs={{0,3},{2,5},{4,7},{6,9},{8,11},{10,13},{12,15},{16,19},{18,21},{20... | collective-permute-start | bytes 196616 | tf_op jit(solution)/shard_map/ppermute | solution.py:85
  11.5 72.2 %collective-permute-start = (bf16[2,2,64,128]{3,2,1,0:T(8,128)(2,1)S(1)}, bf16[2,2,64,128]{3,2,1,0:T(8,128)(2,1)S(1)}, u32[]{:S(2)}, u32[]{:S(2)}) collective-permute-start(bf16[2,2,64,128]{3,2,1,0:T(8,128)(2,1)S(1)} %get-tuple-element.84), channel_id=1, source_target_pairs={{0,1},{2,3},{4,5},{6,7},{8,9},{10,11},{12,13},{14,15},{16,17},{18,... | collective-permute-start | bytes 196616 | tf_op jit(solution)/shard_map/ppermute | solution.py:83
  12.8 71.1 %collective-permute-start.3 = (bf16[2,8,64,128]{3,2,1,0:T(8,128)(2,1)}, bf16[2,8,64,128]{3,2,1,0:T(8,128)(2,1)S(1)}, u32[]{:S(2)}, u32[]{:S(2)}) collective-permute-start(bf16[2,8,64,128]{3,2,1,0:T(8,128)(2,1)} %param.11), channel_id=1, source_target_pairs={{0,2},{1,3},{2,4},{3,5},{4,6},{5,7},{6,8},{7,9},{8,10},{9,11},{10,... | collective-permute-start | bytes 786440 | tf_op jit(solution)/shard_map/ppermute | solution.py:81
  84.1 1.5 %copy-start.2 = (bf16[3,3,3,256,128]{4,3,2,1,0:T(8,128)(2,1)S(1)}, bf16[3,3,3,256,128]{4,3,2,1,0:T(8,128)(2,1)}, u32[]{:S(2)}) copy-start(bf16[3,3,3,256,128]{4,3,2,1,0:T(8,128)(2,1)} %param.14) | copy-start | bytes 5308420
  84.4 1.9 %collective-permute-start.5 = (bf16[4,12,34,128]{3,2,1,0:T(8,128)(2,1)S(1)}, bf16[4,12,34,128]{3,2,1,0:T(8,128)(2,1)S(1)}, u32[]{:S(2)}, u32[]{:S(2)}) collective-permute-start(bf16[4,12,34,128]{3,2,1,0:T(8,128)(2,1)S(1)} %get-tuple-element.55), channel_id=1, source_target_pairs={{0,16},{16,0},{1,17},{17,1},{2,18},{18,2},{3,19},{19,3},{4,20},{20... | collective-permute-start | bytes 1253384 | tf_op jit(solution)/shard_map/ppermute | solution.py:101
  85.7 1.2 %copy-start.11 = (f32[256]{0:T(256)S(1)}, f32[256]{0:T(256)}, u32[]{:S(2)}) copy-start(f32[256]{0:T(256)} %param.13) | copy-start | bytes 3076
  85.7 1.2 %copy-start.12 = (f32[256]{0:T(256)S(1)}, f32[256]{0:T(256)}, u32[]{:S(2)}) copy-start(f32[256]{0:T(256)} %param.12) | copy-start | bytes 3076
  94.2 0.7 copy-start.15
  95.3 12.4 %copy-start.13 = (f32[128]{0:T(128)S(1)}, f32[128]{0:T(128)}, u32[]{:S(2)}) copy-start(f32[128]{0:T(128)} %param.17) | copy-start | bytes 1540
  95.3 12.4 %copy-start.14 = (f32[128]{0:T(128)S(1)}, f32[128]{0:T(128)}, u32[]{:S(2)}) copy-start(f32[128]{0:T(128)} %param.16) | copy-start | bytes 1540
  96.7 9.8 %all-to-all-start = ((f32[32,2,128]{2,1,0:T(2,128)}), f32[32,2,128]{2,1,0:T(2,128)S(1)}, u32[]{:S(2)}, u32[]{:S(2)}) async-start(f32[32,2,128]{2,1,0:T(2,128)} %broadcast_in_dim.163), calls=%async_computation | async-start | bytes 65536 | tf_op jit(solution)/shard_map/all_to_all | solution.py:126
  99.4 8.4 %collective-permute-start.6 = (bf16[2,10,34,128]{3,2,1,0:T(8,128)(2,1)S(1)}, bf16[2,10,34,128]{3,2,1,0:T(8,128)(2,1)S(1)}, u32[]{:S(2)}, u32[]{:S(2)}) collective-permute-start(bf16[2,10,34,128]{3,2,1,0:T(8,128)(2,1)S(1)} %broadcast_select_fusion.6), channel_id=1, source_target_pairs={{0,2},{2,4},{4,6},{6,8},{8,10},{10,12},{12,14},{1,3},{3,5},{5,7},{... | collective-permute-start | bytes 522248 | tf_op jit(solution)/shard_map/ppermute | solution.py:124
  108.2 0.9 copy-start.10
  108.2 1.2 %copy-start.9 = (bf16[1,1,3,128,128]{4,3,2,1,0:T(8,128)(2,1)S(1)}, bf16[1,1,3,128,128]{4,3,2,1,0:T(8,128)(2,1)}, u32[]{:S(2)}) copy-start(bf16[1,1,3,128,128]{4,3,2,1,0:T(8,128)(2,1)} %get-tuple-element.51) | copy-start | bytes 294916
  108.7 1.0 copy-start.8
  109.1 0.9 copy-start.7
  109.4 0.9 copy-start.6
  109.7 0.9 copy-start.5
  110.0 0.9 copy-start.4
  110.6 0.9 copy-start.16
  111.0 0.8 copy-start.17

commit v2 on v1

v2 whole, which is shorter than its diff:
```python
import functools

import jax
import jax.numpy as jnp
from jax import lax
from jax.experimental import pallas as pl
from jax.experimental.pallas import tpu as pltpu
from jax.sharding import PartitionSpec as P

GROUPS = 32
AXES = ("section", "tm", "tile")
VMEM_LIMIT = 48 * 1024 * 1024
RIM = 16


def params():
    return pltpu.CompilerParams(vmem_limit_bytes=VMEM_LIMIT)


def vmem_specs(count):
    return [pl.BlockSpec(memory_space=pltpu.VMEM)] * count


def silu(u):
    half = 0.5 * u
    return half + half * jnp.tanh(half)


def moments_of(cells):
    mean = jnp.sum(cells, axis=0, keepdims=True) * (1.0 / cells.shape[0])
    off = cells - mean
    return jnp.concatenate([mean, jnp.sum(off * off, axis=0, keepdims=True)], axis=0)


def group_matrix(channels, width):
    shape = (channels, channels)
    row = lax.broadcasted_iota(jnp.int32, shape, 0) // width
    col = lax.broadcasted_iota(jnp.int32, shape, 1) // width
    return jnp.where(row == col, 1.0, 0.0).astype(jnp.float32)


def group_sum(values, matrix):
    tall = jnp.broadcast_to(values, (8, values.shape[-1]))
    return jnp.dot(
        tall, matrix, preferred_element_type=jnp.float32, precision=lax.Precision.HIGHEST
    )[:1]


def scale_and_offset(moments, cells, width, gain, shift):
    devices, _, channels = moments.shape
    matrix = group_matrix(channels, width)
    means = moments[:, 0, :]
    spreads = moments[:, 1, :]
    mean = group_sum(jnp.sum(means, axis=0, keepdims=True), matrix) * (1.0 / (devices * width))
    off = means - mean
    total = jnp.sum(spreads + float(cells) * (off * off), axis=0, keepdims=True)
    spread = group_sum(total, matrix) * (1.0 / (cells * devices * width))
    scale = lax.rsqrt(spread + 1e-6) * gain
    return mean, scale, shift


def apply_norm(values, norm):
    mean, scale, shift = norm
    return silu((values.astype(jnp.float32) - mean) * scale + shift).astype(jnp.bfloat16)


def first_kernel(x_ref, moments_ref, top_ref, bottom_ref):
    x = x_ref[...]
    cells = x.astype(jnp.float32).reshape(-1, x.shape[-1])
    own = moments_of(cells)
    moments_ref[...] = jnp.broadcast_to(own[None], moments_ref.shape)
    top_ref[...] = x_ref[:, :2]
    bottom_ref[...] = x_ref[:, -2:]


def conv_rows(act_ref, weight_ref, frame, rows, width):
    total = None
    for t in range(3):
        for h in range(3):
            cells = act_ref[frame + t, h : h + rows]
            cells = cells.reshape(rows * width, cells.shape[-1])
            taps = jnp.concatenate([weight_ref[t, h, w] for w in range(3)], axis=-1)
            part = jnp.dot(cells, taps, preferred_element_type=jnp.float32)
            total = part if total is None else total + part
    outputs = weight_ref.shape[-1]
    total = total.reshape(rows, width, 3 * outputs)
    before, middle, after = (total[..., k * outputs : (k + 1) * outputs] for k in range(3))
    before = jnp.concatenate([before[:, :1], before[:, :-1]], axis=1)
    after = jnp.concatenate([after[:, 1:], after[:, -1:]], axis=1)
    return middle + before + after


def middle_kernel(
    tiles,
    x_ref,
    prev_ref,
    up_ref,
    down_ref,
    up_prev_ref,
    down_prev_ref,
    other_x_ref,
    other_prev_ref,
    other_up_ref,
    other_down_ref,
    other_up_prev_ref,
    other_down_prev_ref,
    moments_ref,
    gain_ref,
    shift_ref,
    weight_ref,
    bias_ref,
    hidden_ref,
    out_moments_ref,
    act_ref,
):
    section, tm, tile = (lax.axis_index(axis) for axis in AXES)
    frames, rows, columns, half = x_ref.shape
    width = columns // 2 + RIM
    first = pl.multiple_of(section * (columns - width), RIM)
    cols = pl.ds(first, width)
    per_section = moments_ref.shape[0] // 2
    pieces = (
        (
            section,
            ((x_ref, up_ref, down_ref), (prev_ref, up_prev_ref, down_prev_ref)),
        ),
        (
            1 - section,
            (
                (other_x_ref, other_up_ref, other_down_ref),
                (other_prev_ref, other_up_prev_ref, other_down_prev_ref),
            ),
        ),
    )
    for which, (now, before) in pieces:
        norm = scale_and_offset(
            moments_ref[pl.ds(which * per_section, per_section)],
            frames * rows * columns,
            2 * half // GROUPS,
            gain_ref[pl.ds(which, 1), :],
            shift_ref[pl.ds(which, 1), :],
        )
        lanes = pl.ds(pl.multiple_of(which * half, half), half)
        for start, (body, up, down) in ((frames, now), (0, before)):
            for f in range(frames):
                act_ref[start + f, 2 : 2 + rows, :, lanes] = apply_norm(body[f, :, cols, :], norm)
                act_ref[start + f, 0:2, :, lanes] = apply_norm(up[f, :, cols, :], norm)
                act_ref[start + f, 2 + rows :, :, lanes] = apply_norm(down[f, :, cols, :], norm)

    @pl.when(tile == 0)
    def _():
        for f in range(2 * frames):
            act_ref[f, 1] = act_ref[f, 2]

    @pl.when(tile == tiles - 1)
    def _():
        for f in range(2 * frames):
            act_ref[f, rows + 2] = act_ref[f, rows + 1]

    @pl.when(tm == 0)
    def _():
        for f in range(frames):
            act_ref[f] = act_ref[frames]

    for f in range(frames):
        hidden = conv_rows(act_ref, weight_ref, f, rows + 2, width) + bias_ref[...]
        hidden_ref[f] = hidden.astype(jnp.bfloat16)

    cells = hidden_ref[:, 1 : 1 + rows, pl.ds(first, columns // 2), :]
    cells = cells.astype(jnp.float32).reshape(-1, cells.shape[-1])
    own = moments_of(cells)
    out_moments_ref[...] = jnp.broadcast_to(own[None], out_moments_ref.shape)


def last_kernel(
    tiles,
    hidden_ref,
    before_ref,
    moments_ref,
    gain_ref,
    shift_ref,
    weight_ref,
    bias_ref,
    x_ref,
    other_x_ref,
    skip_ref,
    skip_bias_ref,
    out_ref,
    act_ref,
):
    section, tm, tile = (lax.axis_index(axis) for axis in AXES)
    frames, padded, width, outputs = hidden_ref.shape
    rows = padded - 2
    columns = x_ref.shape[2]
    half = x_ref.shape[3]
    own = columns // 2
    norm = scale_and_offset(
        moments_ref[...],
        frames * rows * own,
        outputs // GROUPS,
        gain_ref[...],
        shift_ref[...],
    )
    for f in range(frames):
        act_ref[f] = apply_norm(before_ref[f], norm)
        act_ref[frames + f] = apply_norm(hidden_ref[f], norm)

    @pl.when(tile == 0)
    def _():
        for f in range(2 * frames):
            act_ref[f, 0] = act_ref[f, 1]

    @pl.when(tile == tiles - 1)
    def _():
        for f in range(2 * frames):
            act_ref[f, rows + 1] = act_ref[f, rows]

    @pl.when(tm == 0)
    def _():
        for f in range(frames):
            act_ref[f] = act_ref[frames]

    mine = pl.ds(pl.multiple_of(section * own, own), own)
    skip_here = skip_ref[pl.ds(pl.multiple_of(section * half, half), half), :]
    skip_there = skip_ref[pl.ds(pl.multiple_of((1 - section) * half, half), half), :]
    for f in range(frames):
        residual = conv_rows(act_ref, weight_ref, f, rows, width)
        residual = jnp.where(section == 0, residual[:, :own], residual[:, width - own :])
        here = x_ref[f, :, mine, :].reshape(rows * own, half)
        there = other_x_ref[f, :, mine, :].reshape(rows * own, half)
        shortcut = jnp.dot(here, skip_here, preferred_element_type=jnp.float32)
        shortcut = shortcut + jnp.dot(there, skip_there, preferred_element_type=jnp.float32)
        total = (residual + bias_ref[...]) + (
            shortcut.reshape(rows, own, outputs) + skip_bias_ref[...]
        )
        out_ref[f] = total.astype(jnp.bfloat16)


def pairs_for(tm_count, tile_count, tm_step, tile_step):
    out = []
    for a in range(tm_count):
        for b in range(tile_count):
            c, d = a + tm_step, b + tile_step
            if 0 <= c < tm_count and 0 <= d < tile_count:
                out.append((a * tile_count + b, c * tile_count + d))
    return out


def to_everyone(moments):
    return lax.all_to_all(moments, AXES, 0, 0, tiled=True)


def shards(
    features,
    norm_gain_in,
    norm_shift_in,
    conv_in_weight,
    conv_in_bias,
    norm_gain_mid,
    norm_shift_mid,
    conv_mid_weight,
    conv_mid_bias,
    skip_weight,
    skip_bias,
):
    sections, tms, tiles = (lax.axis_size(axis) for axis in AXES)
    devices = sections * tms * tiles
    tile = lax.axis_index("tile")
    frames, rows, columns, half = features.shape
    own = columns // sections
    width = own + RIM
    middle = conv_in_weight.shape[-1]
    outputs = conv_mid_weight.shape[-1]
    grid_axes = ("tm", "tile")

    def shift(value, tm_step, tile_step):
        return lax.ppermute(value, grid_axes, pairs_for(tms, tiles, tm_step, tile_step))

    def swap(value):
        return lax.ppermute(value, "section", [(0, 1), (1, 0)])

    previous = shift(features, 1, 0)
    edge = jax.ShapeDtypeStruct((frames, 2, columns, half), features.dtype)
    moments, top, bottom = pl.pallas_call(
        first_kernel,
        out_shape=(jax.ShapeDtypeStruct((devices, 2, half), jnp.float32), edge, edge),
        in_specs=vmem_specs(1),
        out_specs=tuple(vmem_specs(3)),
        compiler_params=params(),
        name="feature_moments",
    )(features)
    if tiles == 2:
        facing = jnp.where(tile == 0, bottom, top)
        up = down = lax.ppermute(facing, "tile", [(0, 1), (1, 0)])
        crossing = [
            (a * 2 + b, (a + 1) * 2 + 1 - b) for a in range(tms - 1) for b in range(2)
        ]
        up_prev = down_prev = lax.ppermute(facing, grid_axes, crossing)
        rims = [up, up_prev]
        other_up, other_up_prev = (swap(rim) for rim in rims)
        other_down, other_down_prev = other_up, other_up_prev
    else:
        up, down = shift(bottom, 0, 1), shift(top, 0, -1)
        up_prev, down_prev = shift(bottom, 1, 1), shift(top, 1, -1)
        other_up, other_down = swap(up), swap(down)
        other_up_prev, other_down_prev = swap(up_prev), swap(down_prev)
    moments = to_everyone(moments)
    other = swap(features)
    other_previous = swap(previous)

    hidden, moments_mid = pl.pallas_call(
        functools.partial(middle_kernel, tiles),
        out_shape=(
            jax.ShapeDtypeStruct((frames, rows + 2, width, middle), jnp.bfloat16),
            jax.ShapeDtypeStruct((devices, 2, middle), jnp.float32),
        ),
        in_specs=vmem_specs(17),
        out_specs=tuple(vmem_specs(2)),
        scratch_shapes=[pltpu.VMEM((2 * frames, rows + 4, width, 2 * half), jnp.bfloat16)],
        compiler_params=params(),
        name="norm_conv_in",
    )(
        features,
        previous,
        up,
        down,
        up_prev,
        down_prev,
        other,
        other_previous,
        other_up,
        other_down,
        other_up_prev,
        other_down_prev,
        moments,
        norm_gain_in.reshape(2, half),
        norm_shift_in.reshape(2, half),
        conv_in_weight,
        conv_in_bias.reshape(1, middle),
    )
    before = shift(hidden, 1, 0)
    moments_mid = to_everyone(moments_mid)
    return pl.pallas_call(
        functools.partial(last_kernel, tiles),
        out_shape=jax.ShapeDtypeStruct((frames, rows, own, outputs), jnp.bfloat16),
        in_specs=vmem_specs(11),
        out_specs=pl.BlockSpec(memory_space=pltpu.VMEM),
        scratch_shapes=[pltpu.VMEM((2 * frames, rows + 2, width, middle), jnp.bfloat16)],
        compiler_params=params(),
        name="norm_conv_mid",
    )(
        hidden,
        before,
        moments_mid,
        norm_gain_mid.reshape(1, middle),
        norm_shift_mid.reshape(1, middle),
        conv_mid_weight,
        conv_mid_bias.reshape(1, outputs),
        features,
        other,
        skip_weight,
        skip_bias.reshape(1, outputs),
    )


def solution(mesh):
    in_specs = (P("tm", "tile", None, "section"),) + (P(),) * 10
    out_specs = P("tm", "tile", "section", None)
    return jax.shard_map(shards, mesh=mesh, in_specs=in_specs, out_specs=out_specs, check_vma=False)
```

time: 114 us -> 56.6 us (0.50)
  blocking collectives: 63.7 us -> 21.7 us
  starting transfers between devices: 21.7 us -> 13.4 us
  matrix products: 7.95 us -> 0 us
  Pallas kernels: 0 us -> 7.22 us
  other arithmetic: 6 us -> 0.01 us
  waiting for transfers between devices: 4.17 us -> 8.28 us
  local copies, waits for them, and re-layouts: 8.42 us -> 5.41 us
    all_gather x1 -> x0, blocking collectives: 63.7 us -> none  [shards(): gathered = lax.all_gather(local_moments(features), AXES)]
    all_to_all x0 -> x2, blocking collectives: none -> 21.7 us  [to_everyone(): return lax.all_to_all(moments, AXES, 0, 0, tiled=True)]
    dot_general x19 -> x0, matrix products: 7.95 us -> none  [the longest x18 7.05 us: convolve(): jnp.einsum('frck,ko->frco', window, weights[t, h].reshape(3 * channels, o...]
    ppermute x7 -> x8, waiting for transfers between devices: 0.85 us -> 8.28 us  [the longest x2 4.51 us: shift(): lax.ppermute(value, grid_axes, pairs_for(tms, tiles, tm_step, tile_step))]
    pallas_call x0 -> x3, Pallas kernels: none -> 7.22 us  [the longest x1 3.89 us: shards(): pl.pallas_call(functools.partial(middle_kernel, tiles), out_shape=(jax.Sh...]
    ppermute x7 -> x8, starting transfers between devices: 19.1 us -> 13.4 us  [the longest x2 7.42 us: shift(): lax.ppermute(value, grid_axes, pairs_for(tms, tiles, tm_step, tile_step))]
    slice x14 -> x0, local copies, waits for them, and re-layouts: 4.94 us -> none  [the longest x4 2.86 us: convolve(): slab[:, :, w:w + columns]]
    unnamed x39 -> x24, local copies, waits for them, and re-layouts: 1.73 us -> 5.41 us
  transfers between devices with their start and end apart: 8 -> 8, of which waited for: 3 -> 3; matrix products, arithmetic and copies ran while one was open for 4% -> 0% of each run, Pallas kernels for 0% -> 1%
where the time goes in v2:
time: 56.6 us; the launch traced here: 56.3 us
  blocking collectives  21.7 us (38%)
  starting transfers between devices  13.4 us (24%)
  waiting for transfers between devices  8.28 us (15%)
  Pallas kernels  7.22 us (13%)
  local copies, waits for them, and re-layouts  5.41 us (10%)
    all_to_all x2, blocking collectives, to_everyone(): return lax.all_to_all(moments, AXES, 0, 0, tiled=True)  21.7 us
    ppermute x2, starting transfers between devices, shift(): lax.ppermute(value, grid_axes, pairs_for(tms, tiles, tm_step, tile_step))  7.42 us
    unnamed x24, local copies, waits for them, and re-layouts  5.41 us
    ppermute x1, starting transfers between devices, shards(): up_prev = down_prev = lax.ppermute(facing, grid_axes, crossing)  5.37 us
    ppermute x2, waiting for transfers between devices, shift(): lax.ppermute(value, grid_axes, pairs_for(tms, tiles, tm_step, tile_step))  4.51 us
    pallas_call x1, Pallas kernels, shards(): pl.pallas_call(functools.partial(middle_kernel, tiles), out_shape=(jax.Sh...  3.89 us
    pallas_call x1, Pallas kernels, shards(): pl.pallas_call(functools.partial(last_kernel, tiles), out_shape=jax.Shape...  3.04 us
    ppermute x1, waiting for transfers between devices, shards(): up = down = lax.ppermute(facing, 'tile', [(0, 1), (1, 0)])  2.33 us
  transfers between devices with their start and end apart: 8, of which 3 were waited for; matrix products, arithmetic and copies ran while one was open for 0% of the time, Pallas kernels for 1%

profile of v2, /device:TPU:0, one launch (start us, length us, event | category | flops | bytes accessed | tf_op | source)
XLA Modules:
  0.0 56.3 jit_solution(3478746651972448223)
XLA Ops:
  0.0 4.8 %collective-permute-start = (bf16[2,8,64,128]{3,2,1,0:T(8,128)(2,1)}, bf16[2,8,64,128]{3,2,1,0:T(8,128)(2,1)S(1)}, u32[]{:S(2)}, u32[]{:S(2)}) collective-permute-start(bf16[2,8,64,128]{3,2,1,0:T(8,128)(2,1)} %x_ref.5), channel_id=1, source_target_pairs={{0,2},{1,3},{2,4},{3,5},{4,6},{5,7},{6,8},{7,9},{8,10},{9,11},{10,... | collective-permute-start | bytes 786440 | tf_op jit(solution)/shard_map/ppermute | solution.py:277
  4.9 0.1 collective-permute-start.3
  4.9 0.0 copy-start
  5.0 0.9 %copy-done = bf16[2,8,64,128]{3,2,1,0:T(8,128)(2,1)S(1)} copy-done((bf16[2,8,64,128]{3,2,1,0:T(8,128)(2,1)S(1)}, bf16[2,8,64,128]{3,2,1,0:T(8,128)(2,1)}, u32[]{:S(2)}) %copy-start) | copy-done | bytes 262168
  5.9 0.3 feature_moments.1
  6.2 4.5 %collective-permute-done.prev_ref = bf16[2,8,64,128]{3,2,1,0:T(8,128)(2,1)S(1)} collective-permute-done((bf16[2,8,64,128]{3,2,1,0:T(8,128)(2,1)}, bf16[2,8,64,128]{3,2,1,0:T(8,128)(2,1)S(1)}, u32[]{:S(2)}, u32[]{:S(2)}) %collective-permute-start) | collective-permute-done | bytes 262176 | tf_op jit(solution)/shard_map/ppermute | solution.py:277
  10.7 0.0 collective-permute-start.4
  10.7 0.0 copy-start.4
  10.7 0.0 copy-start.8
  10.7 0.0 copy-start.9
  10.8 0.0 copy-start.10
  10.8 0.0 copy-start.11
  10.8 5.4 %collective-permute-start.2 = (bf16[2,2,64,128]{3,2,1,0:T(8,128)(2,1)S(1)}, bf16[2,2,64,128]{3,2,1,0:T(8,128)(2,1)S(1)}, u32[]{:S(2)}, u32[]{:S(2)}) collective-permute-start(bf16[2,2,64,128]{3,2,1,0:T(8,128)(2,1)S(1)} %broadcast_select_fusion), channel_id=1, source_target_pairs={{0,3},{1,2},{2,5},{3,4},{4,7},{5,6},{6,9},{7,8},{8,11},{9,10},{10,... | collective-permute-start | bytes 196616 | tf_op jit(solution)/shard_map/ppermute | solution.py:298
  16.2 0.6 %collective-permute-start.1 = (bf16[2,2,64,128]{3,2,1,0:T(8,128)(2,1)S(1)}, bf16[2,2,64,128]{3,2,1,0:T(8,128)(2,1)S(1)}, u32[]{:S(2)}, u32[]{:S(2)}) collective-permute-start(bf16[2,2,64,128]{3,2,1,0:T(8,128)(2,1)S(1)} %broadcast_select_fusion), channel_id=1, source_target_pairs={{0,1},{1,0},{2,3},{3,2},{4,5},{5,4},{6,7},{7,6},{8,9},{9,8},{10,11... | collective-permute-start | bytes 196616 | tf_op jit(solution)/shard_map/ppermute | solution.py:294
  16.7 1.4 %collective-permute-done.2.up_prev_ref.down_prev_ref = bf16[2,2,64,128]{3,2,1,0:T(8,128)(2,1)S(1)} collective-permute-done((bf16[2,2,64,128]{3,2,1,0:T(8,128)(2,1)S(1)}, bf16[2,2,64,128]{3,2,1,0:T(8,128)(2,1)S(1)}, u32[]{:S(2)}, u32[]{:S(2)}) %collective-permute-start.2) | collective-permute-done | bytes 65568 | tf_op jit(solution)/shard_map/ppermute | solution.py:298
  18.2 0.0 collective-permute-start.6
  18.2 2.3 %collective-permute-done.1.up_ref.down_ref = bf16[2,2,64,128]{3,2,1,0:T(8,128)(2,1)S(1)} collective-permute-done((bf16[2,2,64,128]{3,2,1,0:T(8,128)(2,1)S(1)}, bf16[2,2,64,128]{3,2,1,0:T(8,128)(2,1)S(1)}, u32[]{:S(2)}, u32[]{:S(2)}) %collective-permute-start.1) | collective-permute-done | bytes 65568 | tf_op jit(solution)/shard_map/ppermute | solution.py:294
  20.5 0.0 collective-permute-start.5
  20.5 12.8 %all_to_all.10.moments_ref = f32[32,2,128]{2,1,0:T(2,128)S(1)} all-to-all(f32[32,2,128]{2,1,0:T(2,128)S(1)} %get-tuple-element.12), channel_id=1, replica_groups=mesh['section'=2,'tm'=8,'tile'=2] {'section','tm','tile'}, dimensions={0} | all-to-all | bytes 65536 | tf_op jit(solution)/shard_map/all_to_all | solution.py:250
  33.3 0.0 collective-permute-done.6.other_up_prev_ref.other_down_prev_ref
  33.3 0.0 collective-permute-done.5.other_up_ref.other_down_ref
  33.3 0.0 collective-permute-done.3.other_x_ref
  33.3 0.0 collective-permute-done.4.other_prev_ref
  33.4 0.0 copy-start.1
  33.4 0.9 %copy-done.1 = bf16[2,8,64,128]{3,2,1,0:T(8,128)(2,1)S(1)} copy-done((bf16[2,8,64,128]{3,2,1,0:T(8,128)(2,1)S(1)}, bf16[2,8,64,128]{3,2,1,0:T(8,128)(2,1)}, u32[]{:S(2)}) %copy-start.1) | copy-done | bytes 262168
  34.3 0.0 copy-start.2
  34.3 1.5 %copy-done.2 = bf16[3,3,3,256,128]{4,3,2,1,0:T(8,128)(2,1)S(1)} copy-done((bf16[3,3,3,256,128]{4,3,2,1,0:T(8,128)(2,1)S(1)}, bf16[3,3,3,256,128]{4,3,2,1,0:T(8,128)(2,1)}, u32[]{:S(2)}) %copy-start.2) | copy-done | bytes 1769496
  35.8 0.0 copy-start.5
  35.8 0.7 %copy-done.5 = f32[256]{0:T(256)S(1)} copy-done((f32[256]{0:T(256)S(1)}, f32[256]{0:T(256)}, u32[]{:S(2)}) %copy-start.5) | copy-done | bytes 1048
  36.5 0.0 copy-start.6
  36.5 0.7 %copy-done.6 = f32[256]{0:T(256)S(1)} copy-done((f32[256]{0:T(256)S(1)}, f32[256]{0:T(256)}, u32[]{:S(2)}) %copy-start.6) | copy-done | bytes 1048
  37.1 0.0 copy-start.7
  37.1 0.7 %copy-done.7 = f32[128]{0:T(128)S(1)} copy-done((f32[128]{0:T(128)S(1)}, f32[128]{0:T(128)}, u32[]{:S(2)}) %copy-start.7) | copy-done | bytes 536
  37.8 0.0 copy-start.3
  37.8 3.9 %norm_conv_in.1 = (bf16[2,10,48,128]{3,2,1,0:T(8,128)(2,1)S(1)}, f32[32,2,128]{2,1,0:T(2,128)S(1)}) custom-call(bf16[2,8,64,128]{3,2,1,0:T(8,128)(2,1)S(1)} %copy-done.1, bf16[2,8,64,128]{3,2,1,0:T(8,128)(2,1)S(1)} %collective-permute-done.prev_ref, bf16[2,2,64,128]{3,2,1,0:T(8,128)(2,1)S(1)} %collective-permute-done.1.up_ref.down_ref, ...), custom_call_target="tpu_custom_call" | custom-call | tf_op jit(solution)/shard_map/norm_conv_in/pallas_call | solution.py:311
  41.7 2.6 %collective-permute-start.7 = (bf16[2,10,48,128]{3,2,1,0:T(8,128)(2,1)S(1)}, bf16[2,10,48,128]{3,2,1,0:T(8,128)(2,1)S(1)}, u32[]{:S(2)}, u32[]{:S(2)}) collective-permute-start(bf16[2,10,48,128]{3,2,1,0:T(8,128)(2,1)S(1)} %get-tuple-element.13.hidden_ref), channel_id=1, source_target_pairs={{0,2},{1,3},{2,4},{3,5},{4,6},{5,7},{6,8},{7,9},{8,10},{9,11},{10,... | collective-permute-start | bytes 737288 | tf_op jit(solution)/shard_map/ppermute | solution.py:277
  44.3 8.9 %all_to_all.11.moments_ref = f32[32,2,128]{2,1,0:T(2,128)S(1)} all-to-all(f32[32,2,128]{2,1,0:T(2,128)S(1)} %get-tuple-element.14), channel_id=1, replica_groups=mesh['section'=2,'tm'=8,'tile'=2] {'section','tm','tile'}, dimensions={0} | all-to-all | bytes 65536 | tf_op jit(solution)/shard_map/all_to_all | solution.py:250
  53.2 0.0 collective-permute-done.7.before_ref
  53.2 0.0 copy-done.4
  53.2 0.0 copy-done.8
  53.2 0.0 copy-done.9
  53.2 0.0 copy-done.10
  53.2 0.0 copy-done.11
  53.2 0.0 copy-done.3
  53.2 3.0 %norm_conv_mid.1 = bf16[2,8,32,128]{3,2,1,0:T(8,128)(2,1)} custom-call(bf16[2,10,48,128]{3,2,1,0:T(8,128)(2,1)S(1)} %get-tuple-element.13.hidden_ref, bf16[2,10,48,128]{3,2,1,0:T(8,128)(2,1)S(1)} %collective-permute-done.7.before_ref, f32[32,2,128]{2,1,0:T(2,128)S(1)} %all_to_all.11.moments_ref, f32[1,128]{1,0:T(1,128)S(1)} %bitcast.10, ...), custom_call_target="tpu_custom_call" | custom-call | tf_op jit(solution)/shard_map/norm_conv_mid/pallas_call | solution.py:343
  (1 shorter events, 0.0 us)
Async XLA Ops:
  0.0 10.7 %collective-permute-start = (bf16[2,8,64,128]{3,2,1,0:T(8,128)(2,1)}, bf16[2,8,64,128]{3,2,1,0:T(8,128)(2,1)S(1)}, u32[]{:S(2)}, u32[]{:S(2)}) collective-permute-start(bf16[2,8,64,128]{3,2,1,0:T(8,128)(2,1)} %x_ref.5), channel_id=1, source_target_pairs={{0,2},{1,3},{2,4},{3,5},{4,6},{5,7},{6,8},{7,9},{8,10},{9,11},{10,... | collective-permute-start | bytes 786440 | tf_op jit(solution)/shard_map/ppermute | solution.py:277
  4.9 28.5 %collective-permute-start.3 = (bf16[2,8,64,128]{3,2,1,0:T(8,128)(2,1)}, bf16[2,8,64,128]{3,2,1,0:T(8,128)(2,1)S(1)}, u32[]{:S(2)}, u32[]{:S(2)}) collective-permute-start(bf16[2,8,64,128]{3,2,1,0:T(8,128)(2,1)} %x_ref.5), channel_id=1, source_target_pairs={{0,16},{16,0},{1,17},{17,1},{2,18},{18,2},{3,19},{19,3},{4,20},{20... | collective-permute-start | bytes 786440 | tf_op jit(solution)/shard_map/ppermute | solution.py:280
  4.9 1.0 %copy-start = (bf16[2,8,64,128]{3,2,1,0:T(8,128)(2,1)S(1)}, bf16[2,8,64,128]{3,2,1,0:T(8,128)(2,1)}, u32[]{:S(2)}) copy-start(bf16[2,8,64,128]{3,2,1,0:T(8,128)(2,1)} %x_ref.5) | copy-start | bytes 786436
  10.7 22.6 %collective-permute-start.4 = (bf16[2,8,64,128]{3,2,1,0:T(8,128)(2,1)S(1)}, bf16[2,8,64,128]{3,2,1,0:T(8,128)(2,1)S(1)}, u32[]{:S(2)}, u32[]{:S(2)}) collective-permute-start(bf16[2,8,64,128]{3,2,1,0:T(8,128)(2,1)S(1)} %collective-permute-done.prev_ref), channel_id=1, source_target_pairs={{0,16},{16,0},{1,17},{17,1},{2,18},{18,2},{3,19},{19,3},{4,20},{20... | collective-permute-start | bytes 786440 | tf_op jit(solution)/shard_map/ppermute | solution.py:280
  10.7 42.5 %copy-start.4 = (bf16[256,128]{1,0:T(8,128)(2,1)S(1)}, bf16[256,128]{1,0:T(8,128)(2,1)}, u32[]{:S(2)}) copy-start(bf16[256,128]{1,0:T(8,128)(2,1)} %skip_ref.1) | copy-start | bytes 196612
  10.7 42.5 %copy-start.8 = (f32[128]{0:T(128)S(1)}, f32[128]{0:T(128)}, u32[]{:S(2)}) copy-start(f32[128]{0:T(128)} %param.16) | copy-start | bytes 1540
  10.7 42.5 %copy-start.9 = (f32[128]{0:T(128)S(1)}, f32[128]{0:T(128)}, u32[]{:S(2)}) copy-start(f32[128]{0:T(128)} %param.17) | copy-start | bytes 1540
  10.8 42.5 %copy-start.10 = (f32[128]{0:T(128)S(1)}, f32[128]{0:T(128)}, u32[]{:S(2)}) copy-start(f32[128]{0:T(128)} %param.19) | copy-start | bytes 1540
  10.8 42.5 %copy-start.11 = (f32[128]{0:T(128)S(1)}, f32[128]{0:T(128)}, u32[]{:S(2)}) copy-start(f32[128]{0:T(128)} %param.21) | copy-start | bytes 1540
  10.8 7.4 %collective-permute-start.2 = (bf16[2,2,64,128]{3,2,1,0:T(8,128)(2,1)S(1)}, bf16[2,2,64,128]{3,2,1,0:T(8,128)(2,1)S(1)}, u32[]{:S(2)}, u32[]{:S(2)}) collective-permute-start(bf16[2,2,64,128]{3,2,1,0:T(8,128)(2,1)S(1)} %broadcast_select_fusion), channel_id=1, source_target_pairs={{0,3},{1,2},{2,5},{3,4},{4,7},{5,6},{6,9},{7,8},{8,11},{9,10},{10,... | collective-permute-start | bytes 196616 | tf_op jit(solution)/shard_map/ppermute | solution.py:298
  16.2 4.3 %collective-permute-start.1 = (bf16[2,2,64,128]{3,2,1,0:T(8,128)(2,1)S(1)}, bf16[2,2,64,128]{3,2,1,0:T(8,128)(2,1)S(1)}, u32[]{:S(2)}, u32[]{:S(2)}) collective-permute-start(bf16[2,2,64,128]{3,2,1,0:T(8,128)(2,1)S(1)} %broadcast_select_fusion), channel_id=1, source_target_pairs={{0,1},{1,0},{2,3},{3,2},{4,5},{5,4},{6,7},{7,6},{8,9},{9,8},{10,11... | collective-permute-start | bytes 196616 | tf_op jit(solution)/shard_map/ppermute | solution.py:294
  18.2 15.2 %collective-permute-start.6 = (bf16[2,2,64,128]{3,2,1,0:T(8,128)(2,1)S(1)}, bf16[2,2,64,128]{3,2,1,0:T(8,128)(2,1)S(1)}, u32[]{:S(2)}, u32[]{:S(2)}) collective-permute-start(bf16[2,2,64,128]{3,2,1,0:T(8,128)(2,1)S(1)} %collective-permute-done.2.up_prev_ref.down_prev_ref), channel_id=1, source_target_pairs={{0,16},{16,0},{1,17},{17,1},{2,18},{18,2},{3,19},{19,3},{4,20},{20... | collective-permute-start | bytes 196616 | tf_op jit(solution)/shard_map/ppermute | solution.py:280
  20.5 12.8 %collective-permute-start.5 = (bf16[2,2,64,128]{3,2,1,0:T(8,128)(2,1)S(1)}, bf16[2,2,64,128]{3,2,1,0:T(8,128)(2,1)S(1)}, u32[]{:S(2)}, u32[]{:S(2)}) collective-permute-start(bf16[2,2,64,128]{3,2,1,0:T(8,128)(2,1)S(1)} %collective-permute-done.1.up_ref.down_ref), channel_id=1, source_target_pairs={{0,16},{16,0},{1,17},{17,1},{2,18},{18,2},{3,19},{19,3},{4,20},{20... | collective-permute-start | bytes 196616 | tf_op jit(solution)/shard_map/ppermute | solution.py:280
  33.4 1.0 %copy-start.1 = (bf16[2,8,64,128]{3,2,1,0:T(8,128)(2,1)S(1)}, bf16[2,8,64,128]{3,2,1,0:T(8,128)(2,1)}, u32[]{:S(2)}) copy-start(bf16[2,8,64,128]{3,2,1,0:T(8,128)(2,1)} %x_ref.5) | copy-start | bytes 786436
  34.3 1.5 %copy-start.2 = (bf16[3,3,3,256,128]{4,3,2,1,0:T(8,128)(2,1)S(1)}, bf16[3,3,3,256,128]{4,3,2,1,0:T(8,128)(2,1)}, u32[]{:S(2)}) copy-start(bf16[3,3,3,256,128]{4,3,2,1,0:T(8,128)(2,1)} %weight_ref.2) | copy-start | bytes 5308420
  35.8 0.7 %copy-start.5 = (f32[256]{0:T(256)S(1)}, f32[256]{0:T(256)}, u32[]{:S(2)}) copy-start(f32[256]{0:T(256)} %param.12) | copy-start | bytes 3076
  36.5 0.7 %copy-start.6 = (f32[256]{0:T(256)S(1)}, f32[256]{0:T(256)}, u32[]{:S(2)}) copy-start(f32[256]{0:T(256)} %param.13) | copy-start | bytes 3076
  37.1 0.7 %copy-start.7 = (f32[128]{0:T(128)S(1)}, f32[128]{0:T(128)}, u32[]{:S(2)}) copy-start(f32[128]{0:T(128)} %param.15) | copy-start | bytes 1540
  37.8 15.4 %copy-start.3 = (bf16[3,3,3,128,128]{4,3,2,1,0:T(8,128)(2,1)S(1)}, bf16[3,3,3,128,128]{4,3,2,1,0:T(8,128)(2,1)}, u32[]{:S(2)}) copy-start(bf16[3,3,3,128,128]{4,3,2,1,0:T(8,128)(2,1)} %weight_ref.3) | copy-start | bytes 2654212
  41.7 11.5 %collective-permute-start.7 = (bf16[2,10,48,128]{3,2,1,0:T(8,128)(2,1)S(1)}, bf16[2,10,48,128]{3,2,1,0:T(8,128)(2,1)S(1)}, u32[]{:S(2)}, u32[]{:S(2)}) collective-permute-start(bf16[2,10,48,128]{3,2,1,0:T(8,128)(2,1)S(1)} %get-tuple-element.13.hidden_ref), channel_id=1, source_target_pairs={{0,2},{1,3},{2,4},{3,5},{4,6},{5,7},{6,8},{7,9},{8,10},{9,11},{10,... | collective-permute-start | bytes 737288 | tf_op jit(solution)/shard_map/ppermute | solution.py:277

commit v3 on v2

--- a/solution.py
+++ b/solution.py
@@ -15,6 +15,10 @@
 
 def params():
     return pltpu.CompilerParams(vmem_limit_bytes=VMEM_LIMIT)
+
+
+def cost(flops, moved):
+    return pl.CostEstimate(flops=flops, bytes_accessed=moved, transcendentals=0)
 
 
 def vmem_specs(count):
@@ -105,10 +109,8 @@
     other_up_prev_ref,
     other_down_prev_ref,
     moments_ref,
-    gain_ref,
-    shift_ref,
+    vectors_ref,
     weight_ref,
-    bias_ref,
     hidden_ref,
     out_moments_ref,
     act_ref,
@@ -137,8 +139,8 @@
             moments_ref[pl.ds(which * per_section, per_section)],
             frames * rows * columns,
             2 * half // GROUPS,
-            gain_ref[pl.ds(which, 1), :],
-            shift_ref[pl.ds(which, 1), :],
+            vectors_ref[pl.ds(which, 1), :],
+            vectors_ref[pl.ds(2 + which, 1), :],
         )
         lanes = pl.ds(pl.multiple_of(which * half, half), half)
         for start, (body, up, down) in ((frames, now), (0, before)):
@@ -163,7 +165,7 @@
             act_ref[f] = act_ref[frames]
 
     for f in range(frames):
-        hidden = conv_rows(act_ref, weight_ref, f, rows + 2, width) + bias_ref[...]
+        hidden = conv_rows(act_ref, weight_ref, f, rows + 2, width) + vectors_ref[4:5]
         hidden_ref[f] = hidden.astype(jnp.bfloat16)
 
     cells = hidden_ref[:, 1 : 1 + rows, pl.ds(first, columns // 2), :]
@@ -177,14 +179,11 @@
     hidden_ref,
     before_ref,
     moments_ref,
-    gain_ref,
-    shift_ref,
+    vectors_ref,
     weight_ref,
-    bias_ref,
     x_ref,
     other_x_ref,
     skip_ref,
-    skip_bias_ref,
     out_ref,
     act_ref,
 ):
@@ -198,8 +197,8 @@
         moments_ref[...],
         frames * rows * own,
         outputs // GROUPS,
-        gain_ref[...],
-        shift_ref[...],
+        vectors_ref[5:6],
+        vectors_ref[6:7],
     )
     for f in range(frames):
         act_ref[f] = apply_norm(before_ref[f], norm)
@@ -230,8 +229,8 @@
         there = other_x_ref[f, :, mine, :].reshape(rows * own, half)
         shortcut = jnp.dot(here, skip_here, preferred_element_type=jnp.float32)
         shortcut = shortcut + jnp.dot(there, skip_there, preferred_element_type=jnp.float32)
-        total = (residual + bias_ref[...]) + (
-            shortcut.reshape(rows, own, outputs) + skip_bias_ref[...]
+        total = (residual + vectors_ref[7:8]) + (
+            shortcut.reshape(rows, own, outputs) + vectors_ref[8:9]
         )
         out_ref[f] = total.astype(jnp.bfloat16)
 
@@ -287,26 +286,43 @@
         in_specs=vmem_specs(1),
         out_specs=tuple(vmem_specs(3)),
         compiler_params=params(),
+        cost_estimate=cost(1_000_000_000, 1_000_000),
         name="feature_moments",
     )(features)
+    vectors = jnp.concatenate(
+        [
+            norm_gain_in,
+            norm_shift_in,
+            conv_in_bias,
+            norm_gain_mid,
+            norm_shift_mid,
+            conv_mid_bias,
+            skip_bias,
+        ]
+    ).reshape(-1, half)
     if tiles == 2:
         facing = jnp.where(tile == 0, bottom, top)
-        up = down = lax.ppermute(facing, "tile", [(0, 1), (1, 0)])
         crossing = [
             (a * 2 + b, (a + 1) * 2 + 1 - b) for a in range(tms - 1) for b in range(2)
         ]
-        up_prev = down_prev = lax.ppermute(facing, grid_axes, crossing)
-        rims = [up, up_prev]
-        other_up, other_up_prev = (swap(rim) for rim in rims)
-        other_down, other_down_prev = other_up, other_up_prev
+        rims = [
+            lax.ppermute(facing, "tile", [(0, 1), (1, 0)]),
+            lax.ppermute(facing, grid_axes, crossing),
+        ]
     else:
-        up, down = shift(bottom, 0, 1), shift(top, 0, -1)
-        up_prev, down_prev = shift(bottom, 1, 1), shift(top, 1, -1)
-        other_up, other_down = swap(up), swap(down)
-        other_up_prev, other_down_prev = swap(up_prev), swap(down_prev)
+        rims = [
+            shift(bottom, 0, 1),
+            shift(bottom, 1, 1),
+            shift(top, 0, -1),
+            shift(top, 1, -1),
+        ]
+    other = swap(features)
     moments = to_everyone(moments)
-    other = swap(features)
+    previous, moments, *rims = lax.optimization_barrier((previous, moments, *rims))
     other_previous = swap(previous)
+    other_rims = [swap(rim) for rim in rims]
+    up, up_prev, down, down_prev = (rims * 2)[:4]
+    other_up, other_up_prev, other_down, other_down_prev = (other_rims * 2)[:4]
 
     hidden, moments_mid = pl.pallas_call(
         functools.partial(middle_kernel, tiles),
@@ -314,7 +330,7 @@
             jax.ShapeDtypeStruct((frames, rows + 2, width, middle), jnp.bfloat16),
             jax.ShapeDtypeStruct((devices, 2, middle), jnp.float32),
         ),
-        in_specs=vmem_specs(17),
+        in_specs=vmem_specs(15),
         out_specs=tuple(vmem_specs(2)),
         scratch_shapes=[pltpu.VMEM((2 * frames, rows + 4, width, 2 * half), jnp.bfloat16)],
         compiler_params=params(),
@@ -333,17 +349,15 @@
         other_up_prev,
         other_down_prev,
         moments,
-        norm_gain_in.reshape(2, half),
-        norm_shift_in.reshape(2, half),
+        vectors,
         conv_in_weight,
-        conv_in_bias.reshape(1, middle),
     )
     before = shift(hidden, 1, 0)
     moments_mid = to_everyone(moments_mid)
     return pl.pallas_call(
         functools.partial(last_kernel, tiles),
         out_shape=jax.ShapeDtypeStruct((frames, rows, own, outputs), jnp.bfloat16),
-        in_specs=vmem_specs(11),
+        in_specs=vmem_specs(8),
         out_specs=pl.BlockSpec(memory_space=pltpu.VMEM),
         scratch_shapes=[pltpu.VMEM((2 * frames, rows + 2, width, middle), jnp.bfloat16)],
         compiler_params=params(),
@@ -352,14 +366,11 @@
         hidden,
         before,
         moments_mid,
-        norm_gain_mid.reshape(1, middle),
-        norm_shift_mid.reshape(1, middle),
+        vectors,
         conv_mid_weight,
-        conv_mid_bias.reshape(1, outputs),
         features,
         other,
         skip_weight,
-        skip_bias.reshape(1, outputs),
     )
 
 

time: 56.6 us -> 47.1 us (0.83)
  blocking collectives: 21.7 us -> 9.23 us
  starting transfers between devices: 13.4 us -> 17.9 us
  waiting for transfers between devices: 8.28 us -> 6.42 us
  local copies, waits for them, and re-layouts: 5.41 us -> 4.29 us
  Pallas kernels: 7.22 us -> 8.1 us
  other arithmetic: 0.01 us -> 0.64 us
    all_to_all x2 -> x1, blocking collectives: 21.7 us -> 9.23 us  [to_everyone(): return lax.all_to_all(moments, AXES, 0, 0, tiled=True)]
    all_to_all x0 -> x1, waiting for transfers between devices: none -> 5.83 us  [to_everyone(): return lax.all_to_all(moments, AXES, 0, 0, tiled=True)]
    all_to_all x0 -> x1, starting transfers between devices: none -> 4.83 us  [to_everyone(): return lax.all_to_all(moments, AXES, 0, 0, tiled=True)]
    ppermute x2, waiting for transfers between devices: 4.51 us -> 0.01 us  [shift(): lax.ppermute(value, grid_axes, pairs_for(tms, tiles, tm_step, tile_step))]
    ppermute x2, waiting for transfers between devices: 3.76 us -> 0.01 us  [the longest x1 0.01 us: shards(): lax.ppermute(facing, 'tile', [(0, 1), (1, 0)])]
    unnamed x24 -> x22, local copies, waits for them, and re-layouts: 5.41 us -> 3.63 us
    ppermute x2, starting transfers between devices: 7.42 us -> 6.03 us  [shift(): lax.ppermute(value, grid_axes, pairs_for(tms, tiles, tm_step, tile_step))]
    pallas_call x1, Pallas kernels: 3.89 us -> 4.78 us  [shards(): pl.pallas_call(functools.partial(middle_kernel, tiles), out_shape=(jax.Sh...]
  transfers between devices with their start and end apart: 8 -> 9, of which waited for: 3 -> 3; matrix products, arithmetic and copies ran while one was open for 0% -> 7% of each run, Pallas kernels for 1% -> 0%
where the time goes in v3:
time: 47.1 us; the launch traced here: 46.8 us
  starting transfers between devices  17.9 us (38%)
  blocking collectives  9.23 us (20%)
  Pallas kernels  8.1 us (17%)
  waiting for transfers between devices  6.42 us (14%)
  local copies, waits for them, and re-layouts  4.29 us (9%)
  other arithmetic  0.64 us (1%)
    all_to_all x1, blocking collectives, to_everyone(): return lax.all_to_all(moments, AXES, 0, 0, tiled=True)  9.23 us
    ppermute x2, starting transfers between devices, shift(): lax.ppermute(value, grid_axes, pairs_for(tms, tiles, tm_step, tile_step))  6.03 us
    ppermute x1, starting transfers between devices, shards(): lax.ppermute(facing, grid_axes, crossing)  5.92 us
    all_to_all x1, waiting for transfers between devices, to_everyone(): return lax.all_to_all(moments, AXES, 0, 0, tiled=True)  5.83 us
    all_to_all x1, starting transfers between devices, to_everyone(): return lax.all_to_all(moments, AXES, 0, 0, tiled=True)  4.83 us
    pallas_call x1, Pallas kernels, shards(): pl.pallas_call(functools.partial(middle_kernel, tiles), out_shape=(jax.Sh...  4.78 us
    unnamed x22, local copies, waits for them, and re-layouts  3.63 us
    pallas_call x1, Pallas kernels, shards(): pl.pallas_call(functools.partial(last_kernel, tiles), out_shape=jax.Shape...  3.03 us
  transfers between devices with their start and end apart: 9, of which 3 were waited for; matrix products, arithmetic and copies ran while one was open for 7% of the time, Pallas kernels for 0%

profile of v3, /device:TPU:0, one launch (start us, length us, event | category | flops | bytes accessed | tf_op | source)
XLA Modules:
  0.0 46.8 jit_solution(297523448596916778)
XLA Ops:
  0.0 0.0 copy-start.1
  0.0 0.9 %copy-done.1 = bf16[2,8,64,128]{3,2,1,0:T(8,128)(2,1)S(1)} copy-done((bf16[2,8,64,128]{3,2,1,0:T(8,128)(2,1)S(1)}, bf16[2,8,64,128]{3,2,1,0:T(8,128)(2,1)}, u32[]{:S(2)}) %copy-start.1) | copy-done | bytes 262168
  1.0 0.0 copy-start.2
  1.0 0.0 copy-start.6
  1.0 0.0 copy-start.7
  1.0 0.0 copy-start
  1.0 0.3 feature_moments.1
  1.3 0.0 copy-start.5
  1.3 0.6 %broadcast_select_fusion = bf16[2,2,64,128]{3,2,1,0:T(8,128)(2,1)} fusion(bf16[2,2,64,128]{3,2,1,0:T(8,128)(2,1)S(1)} %get-tuple-element.15, bf16[2,2,64,128]{3,2,1,0:T(8,128)(2,1)S(1)} %get-tuple-element.16, pred[]{:T(512)S(6)} %eq.3), kind=kLoop, calls=%fused_computation | loop fusion | flops 32768 | bytes 196609 | tf_op jit(solution)/shard_map/jit(_where)/select_n | solution.py:304
  1.9 0.0 copy-start.3
  1.9 5.9 %collective-permute-start.2 = (bf16[2,2,64,128]{3,2,1,0:T(8,128)(2,1)}, bf16[2,2,64,128]{3,2,1,0:T(8,128)(2,1)S(1)}, u32[]{:S(2)}, u32[]{:S(2)}) collective-permute-start(bf16[2,2,64,128]{3,2,1,0:T(8,128)(2,1)} %broadcast_select_fusion), channel_id=1, source_target_pairs={{0,3},{1,2},{2,5},{3,4},{4,7},{5,6},{6,9},{7,8},{8,11},{9,10},{10,... | collective-permute-start | bytes 196616 | tf_op jit(solution)/shard_map/ppermute | solution.py:310
  7.8 0.0 copy-done.5
  7.9 0.6 %collective-permute-start.1 = (bf16[2,2,64,128]{3,2,1,0:T(8,128)(2,1)}, bf16[2,2,64,128]{3,2,1,0:T(8,128)(2,1)}, u32[]{:S(2)}, u32[]{:S(2)}) collective-permute-start(bf16[2,2,64,128]{3,2,1,0:T(8,128)(2,1)} %broadcast_select_fusion), channel_id=1, source_target_pairs={{0,1},{1,0},{2,3},{3,2},{4,5},{5,4},{6,7},{7,6},{8,9},{9,8},{10,11... | collective-permute-start | bytes 196616 | tf_op jit(solution)/shard_map/ppermute | solution.py:309
  8.4 0.0 copy-done.2
  8.4 0.0 collective-permute-start.3
  8.4 3.5 %collective-permute-start = (bf16[2,8,64,128]{3,2,1,0:T(8,128)(2,1)S(1)}, bf16[2,8,64,128]{3,2,1,0:T(8,128)(2,1)S(1)}, u32[]{:S(2)}, u32[]{:S(2)}) collective-permute-start(bf16[2,8,64,128]{3,2,1,0:T(8,128)(2,1)S(1)} %copy-done.2), channel_id=1, source_target_pairs={{0,2},{1,3},{2,4},{3,5},{4,6},{5,7},{6,8},{7,9},{8,10},{9,11},{10,... | collective-permute-start | bytes 786440 | tf_op jit(solution)/shard_map/ppermute | solution.py:276
  11.9 4.8 %all-to-all-start = ((f32[32,2,128]{2,1,0:T(2,128)}), f32[32,2,128]{2,1,0:T(2,128)S(1)}, u32[]{:S(2)}, u32[]{:S(2)}) async-start(f32[32,2,128]{2,1,0:T(2,128)} %copy-done.5), calls=%async_computation | async-start | bytes 65536 | tf_op jit(solution)/shard_map/all_to_all | solution.py:249
  16.7 0.0 copy-done.6
  16.8 0.0 copy-done.7
  16.8 0.7 %constant_dynamic-update-slice_fusion.4 = f32[1152]{0:T(1024)S(1)} fusion(f32[1152]{0:T(1024)S(1)} %constant_dynamic-update-slice_fusion.5, f32[128]{0:T(128)} %param.15), kind=kLoop, calls=%fused_computation.5 | loop fusion | bytes 1024
  17.5 0.7 %constant_dynamic-update-slice_fusion.3 = f32[1152]{0:T(1024)S(1)} fusion(f32[1152]{0:T(1024)S(1)} %constant_dynamic-update-slice_fusion.4, f32[128]{0:T(128)} %param.16), kind=kLoop, calls=%fused_computation.4 | loop fusion | bytes 1024
  18.1 5.8 %all-to-all-done.moments_ref = f32[32,2,128]{2,1,0:T(2,128)S(1)} async-done(((f32[32,2,128]{2,1,0:T(2,128)}), f32[32,2,128]{2,1,0:T(2,128)S(1)}, u32[]{:S(2)}, u32[]{:S(2)}) %all-to-all-start) | async-done | bytes 32800 | tf_op jit(solution)/shard_map/all_to_all | solution.py:249
  23.9 0.0 copy-start.4
  23.9 0.0 collective-permute-done.2.up_prev_ref.down_prev_ref
  24.0 0.0 collective-permute-done.1.up_ref.down_ref
  24.0 0.0 collective-permute-done.prev_ref
  24.0 0.1 collective-permute-start.4
  24.0 0.7 %constant_dynamic-update-slice_fusion.2 = f32[1152]{0:T(1024)S(1)} fusion(f32[1152]{0:T(1024)S(1)} %constant_dynamic-update-slice_fusion.3, f32[128]{0:T(128)} %param.17), kind=kLoop, calls=%fused_computation.3 | loop fusion | bytes 1024
  24.7 0.7 %constant_dynamic-update-slice_fusion.1 = f32[1152]{0:T(1024)S(1)} fusion(f32[1152]{0:T(1024)S(1)} %constant_dynamic-update-slice_fusion.2, f32[128]{0:T(128)} %param.19), kind=kLoop, calls=%fused_computation.2 | loop fusion | bytes 1024
  25.4 0.5 %collective-permute-start.5 = (bf16[2,2,64,128]{3,2,1,0:T(8,128)(2,1)}, bf16[2,2,64,128]{3,2,1,0:T(8,128)(2,1)S(1)}, u32[]{:S(2)}, u32[]{:S(2)}) collective-permute-start(bf16[2,2,64,128]{3,2,1,0:T(8,128)(2,1)} %collective-permute-done.1.up_ref.down_ref), channel_id=1, source_target_pairs={{0,16},{16,0},{1,17},{17,1},{2,18},{18,2},{3,19},{19,3},{4,20},{20... | collective-permute-start | bytes 196616 | tf_op jit(solution)/shard_map/ppermute | solution.py:279
  25.9 0.0 collective-permute-start.6
  25.9 0.7 %constant_dynamic-update-slice_fusion = f32[1152]{0:T(1024)S(1)} fusion(f32[1152]{0:T(1024)S(1)} %constant_dynamic-update-slice_fusion.1, f32[128]{0:T(128)} %param.21), kind=kLoop, calls=%fused_computation.1 | loop fusion | bytes 1024 | tf_op jit(solution)/shard_map/concatenate | solution.py:292
  26.5 0.0 collective-permute-done.3.other_x_ref
  26.5 0.4 collective-permute-done.5.other_up_ref.other_down_ref
  27.0 0.1 collective-permute-done.6.other_up_prev_ref.other_down_prev_ref
  27.1 0.0 collective-permute-done.4.other_prev_ref
  27.1 0.0 copy-done
  27.1 4.8 %norm_conv_in.1 = (bf16[2,10,48,128]{3,2,1,0:T(8,128)(2,1)S(1)}, f32[32,2,128]{2,1,0:T(2,128)S(1)}) custom-call(bf16[2,8,64,128]{3,2,1,0:T(8,128)(2,1)S(1)} %copy-done.2, bf16[2,8,64,128]{3,2,1,0:T(8,128)(2,1)S(1)} %collective-permute-done.prev_ref, bf16[2,2,64,128]{3,2,1,0:T(8,128)(2,1)} %collective-permute-done.1.up_ref.down_ref, ...), custom_call_target="tpu_custom_call" | custom-call | tf_op jit(solution)/shard_map/norm_conv_in/pallas_call | solution.py:327
  31.9 2.6 %collective-permute-start.7 = (bf16[2,10,48,128]{3,2,1,0:T(8,128)(2,1)S(1)}, bf16[2,10,48,128]{3,2,1,0:T(8,128)(2,1)S(1)}, u32[]{:S(2)}, u32[]{:S(2)}) collective-permute-start(bf16[2,10,48,128]{3,2,1,0:T(8,128)(2,1)S(1)} %get-tuple-element.21.hidden_ref), channel_id=1, source_target_pairs={{0,2},{1,3},{2,4},{3,5},{4,6},{5,7},{6,8},{7,9},{8,10},{9,11},{10,... | collective-permute-start | bytes 737288 | tf_op jit(solution)/shard_map/ppermute | solution.py:276
  34.5 9.2 %all_to_all.10.moments_ref = f32[32,2,128]{2,1,0:T(2,128)S(1)} all-to-all(f32[32,2,128]{2,1,0:T(2,128)S(1)} %get-tuple-element.22), channel_id=1, replica_groups=mesh['section'=2,'tm'=8,'tile'=2] {'section','tm','tile'}, dimensions={0} | all-to-all | bytes 65536 | tf_op jit(solution)/shard_map/all_to_all | solution.py:249
  43.7 0.0 collective-permute-done.7.before_ref
  43.7 0.0 copy-done.3
  43.7 0.0 copy-done.4
  43.7 3.0 %norm_conv_mid.1 = bf16[2,8,32,128]{3,2,1,0:T(8,128)(2,1)} custom-call(bf16[2,10,48,128]{3,2,1,0:T(8,128)(2,1)S(1)} %get-tuple-element.21.hidden_ref, bf16[2,10,48,128]{3,2,1,0:T(8,128)(2,1)S(1)} %collective-permute-done.7.before_ref, f32[32,2,128]{2,1,0:T(2,128)S(1)} %all_to_all.10.moments_ref, f32[9,128]{1,0:T(8,128)S(1)} %bitcast.2, ...), custom_call_target="tpu_custom_call" | custom-call | tf_op jit(solution)/shard_map/norm_conv_mid/pallas_call | solution.py:357
  (3 shorter events, 0.0 us)
Async XLA Ops:
  0.0 0.9 %copy-start.1 = (bf16[2,8,64,128]{3,2,1,0:T(8,128)(2,1)S(1)}, bf16[2,8,64,128]{3,2,1,0:T(8,128)(2,1)}, u32[]{:S(2)}) copy-start(bf16[2,8,64,128]{3,2,1,0:T(8,128)(2,1)} %x_ref.5) | copy-start | bytes 786436
  1.0 7.5 %copy-start.2 = (bf16[2,8,64,128]{3,2,1,0:T(8,128)(2,1)S(1)}, bf16[2,8,64,128]{3,2,1,0:T(8,128)(2,1)}, u32[]{:S(2)}) copy-start(bf16[2,8,64,128]{3,2,1,0:T(8,128)(2,1)} %x_ref.5) | copy-start | bytes 786436
  1.0 15.8 %copy-start.6 = (f32[256]{0:T(256)S(1)}, f32[256]{0:T(256)}, u32[]{:S(2)}) copy-start(f32[256]{0:T(256)} %param.12) | copy-start | bytes 3076
  1.0 15.8 %copy-start.7 = (f32[256]{0:T(256)S(1)}, f32[256]{0:T(256)}, u32[]{:S(2)}) copy-start(f32[256]{0:T(256)} %param.13) | copy-start | bytes 3076
  1.0 26.2 %copy-start = (bf16[3,3,3,256,128]{4,3,2,1,0:T(8,128)(2,1)S(1)}, bf16[3,3,3,256,128]{4,3,2,1,0:T(8,128)(2,1)}, u32[]{:S(2)}) copy-start(bf16[3,3,3,256,128]{4,3,2,1,0:T(8,128)(2,1)} %weight_ref.2) | copy-start | bytes 5308420
  1.3 6.6 %copy-start.5 = (f32[32,2,128]{2,1,0:T(2,128)}, f32[32,2,128]{2,1,0:T(2,128)S(1)}, u32[]{:S(2)}) copy-start(f32[32,2,128]{2,1,0:T(2,128)S(1)} %get-tuple-element.14) | copy-start | bytes 98308
  1.9 41.8 %copy-start.3 = (bf16[3,3,3,128,128]{4,3,2,1,0:T(8,128)(2,1)S(1)}, bf16[3,3,3,128,128]{4,3,2,1,0:T(8,128)(2,1)}, u32[]{:S(2)}) copy-start(bf16[3,3,3,128,128]{4,3,2,1,0:T(8,128)(2,1)} %weight_ref.3) | copy-start | bytes 2654212
  1.9 22.0 %collective-permute-start.2 = (bf16[2,2,64,128]{3,2,1,0:T(8,128)(2,1)}, bf16[2,2,64,128]{3,2,1,0:T(8,128)(2,1)S(1)}, u32[]{:S(2)}, u32[]{:S(2)}) collective-permute-start(bf16[2,2,64,128]{3,2,1,0:T(8,128)(2,1)} %broadcast_select_fusion), channel_id=1, source_target_pairs={{0,3},{1,2},{2,5},{3,4},{4,7},{5,6},{6,9},{7,8},{8,11},{9,10},{10,... | collective-permute-start | bytes 196616 | tf_op jit(solution)/shard_map/ppermute | solution.py:310
  7.9 16.1 %collective-permute-start.1 = (bf16[2,2,64,128]{3,2,1,0:T(8,128)(2,1)}, bf16[2,2,64,128]{3,2,1,0:T(8,128)(2,1)}, u32[]{:S(2)}, u32[]{:S(2)}) collective-permute-start(bf16[2,2,64,128]{3,2,1,0:T(8,128)(2,1)} %broadcast_select_fusion), channel_id=1, source_target_pairs={{0,1},{1,0},{2,3},{3,2},{4,5},{5,4},{6,7},{7,6},{8,9},{9,8},{10,11... | collective-permute-start | bytes 196616 | tf_op jit(solution)/shard_map/ppermute | solution.py:309
  8.4 18.1 %collective-permute-start.3 = (bf16[2,8,64,128]{3,2,1,0:T(8,128)(2,1)S(1)}, bf16[2,8,64,128]{3,2,1,0:T(8,128)(2,1)S(1)}, u32[]{:S(2)}, u32[]{:S(2)}) collective-permute-start(bf16[2,8,64,128]{3,2,1,0:T(8,128)(2,1)S(1)} %copy-done.2), channel_id=1, source_target_pairs={{0,16},{16,0},{1,17},{17,1},{2,18},{18,2},{3,19},{19,3},{4,20},{20... | collective-permute-start | bytes 786440 | tf_op jit(solution)/shard_map/ppermute | solution.py:279
  8.4 15.5 %collective-permute-start = (bf16[2,8,64,128]{3,2,1,0:T(8,128)(2,1)S(1)}, bf16[2,8,64,128]{3,2,1,0:T(8,128)(2,1)S(1)}, u32[]{:S(2)}, u32[]{:S(2)}) collective-permute-start(bf16[2,8,64,128]{3,2,1,0:T(8,128)(2,1)S(1)} %copy-done.2), channel_id=1, source_target_pairs={{0,2},{1,3},{2,4},{3,5},{4,6},{5,7},{6,8},{7,9},{8,10},{9,11},{10,... | collective-permute-start | bytes 786440 | tf_op jit(solution)/shard_map/ppermute | solution.py:276
  11.9 12.0 %all-to-all-start = ((f32[32,2,128]{2,1,0:T(2,128)}), f32[32,2,128]{2,1,0:T(2,128)S(1)}, u32[]{:S(2)}, u32[]{:S(2)}) async-start(f32[32,2,128]{2,1,0:T(2,128)} %copy-done.5), calls=%async_computation | async-start | bytes 65536 | tf_op jit(solution)/shard_map/all_to_all | solution.py:249
  23.9 19.8 %copy-start.4 = (bf16[256,128]{1,0:T(8,128)(2,1)S(1)}, bf16[256,128]{1,0:T(8,128)(2,1)}, u32[]{:S(2)}) copy-start(bf16[256,128]{1,0:T(8,128)(2,1)} %skip_ref.1) | copy-start | bytes 196612
  24.0 3.2 %collective-permute-start.4 = (bf16[2,8,64,128]{3,2,1,0:T(8,128)(2,1)S(1)}, bf16[2,8,64,128]{3,2,1,0:T(8,128)(2,1)S(1)}, u32[]{:S(2)}, u32[]{:S(2)}) collective-permute-start(bf16[2,8,64,128]{3,2,1,0:T(8,128)(2,1)S(1)} %collective-permute-done.prev_ref), channel_id=1, source_target_pairs={{0,16},{16,0},{1,17},{17,1},{2,18},{18,2},{3,19},{19,3},{4,20},{20... | collective-permute-start | bytes 786440 | tf_op jit(solution)/shard_map/ppermute | solution.py:279
  25.4 1.6 %collective-permute-start.5 = (bf16[2,2,64,128]{3,2,1,0:T(8,128)(2,1)}, bf16[2,2,64,128]{3,2,1,0:T(8,128)(2,1)S(1)}, u32[]{:S(2)}, u32[]{:S(2)}) collective-permute-start(bf16[2,2,64,128]{3,2,1,0:T(8,128)(2,1)} %collective-permute-done.1.up_ref.down_ref), channel_id=1, source_target_pairs={{0,16},{16,0},{1,17},{17,1},{2,18},{18,2},{3,19},{19,3},{4,20},{20... | collective-permute-start | bytes 196616 | tf_op jit(solution)/shard_map/ppermute | solution.py:279
  25.9 1.3 %collective-permute-start.6 = (bf16[2,2,64,128]{3,2,1,0:T(8,128)(2,1)S(1)}, bf16[2,2,64,128]{3,2,1,0:T(8,128)(2,1)S(1)}, u32[]{:S(2)}, u32[]{:S(2)}) collective-permute-start(bf16[2,2,64,128]{3,2,1,0:T(8,128)(2,1)S(1)} %collective-permute-done.2.up_prev_ref.down_prev_ref), channel_id=1, source_target_pairs={{0,16},{16,0},{1,17},{17,1},{2,18},{18,2},{3,19},{19,3},{4,20},{20... | collective-permute-start | bytes 196616 | tf_op jit(solution)/shard_map/ppermute | solution.py:279
  31.9 11.8 %collective-permute-start.7 = (bf16[2,10,48,128]{3,2,1,0:T(8,128)(2,1)S(1)}, bf16[2,10,48,128]{3,2,1,0:T(8,128)(2,1)S(1)}, u32[]{:S(2)}, u32[]{:S(2)}) collective-permute-start(bf16[2,10,48,128]{3,2,1,0:T(8,128)(2,1)S(1)} %get-tuple-element.21.hidden_ref), channel_id=1, source_target_pairs={{0,2},{1,3},{2,4},{3,5},{4,6},{5,7},{6,8},{7,9},{8,10},{9,11},{10,... | collective-permute-start | bytes 737288 | tf_op jit(solution)/shard_map/ppermute | solution.py:276

commit v4 on v2

--- a/solution.py
+++ b/solution.py
@@ -15,6 +15,10 @@
 
 def params():
     return pltpu.CompilerParams(vmem_limit_bytes=VMEM_LIMIT)
+
+
+def cost(flops, moved):
+    return pl.CostEstimate(flops=flops, bytes_accessed=moved, transcendentals=0)
 
 
 def vmem_specs(count):
@@ -64,13 +68,18 @@
     return silu((values.astype(jnp.float32) - mean) * scale + shift).astype(jnp.bfloat16)
 
 
-def first_kernel(x_ref, moments_ref, top_ref, bottom_ref):
+def first_kernel(pairs, x_ref, moments_ref, *edge_refs):
     x = x_ref[...]
     cells = x.astype(jnp.float32).reshape(-1, x.shape[-1])
     own = moments_of(cells)
     moments_ref[...] = jnp.broadcast_to(own[None], moments_ref.shape)
-    top_ref[...] = x_ref[:, :2]
-    bottom_ref[...] = x_ref[:, -2:]
+    rows = x_ref.shape[1]
+    if pairs:
+        first = (rows - 2) * (1 - lax.axis_index("tile"))
+        edge_refs[0][...] = x_ref[:, pl.ds(first, 2)]
+    else:
+        edge_refs[0][...] = x_ref[:, :2]
+        edge_refs[1][...] = x_ref[:, -2:]
 
 
 def conv_rows(act_ref, weight_ref, frame, rows, width):
@@ -265,7 +274,6 @@
 ):
     sections, tms, tiles = (lax.axis_size(axis) for axis in AXES)
     devices = sections * tms * tiles
-    tile = lax.axis_index("tile")
     frames, rows, columns, half = features.shape
     own = columns // sections
     width = own + RIM
@@ -281,32 +289,40 @@
 
     previous = shift(features, 1, 0)
     edge = jax.ShapeDtypeStruct((frames, 2, columns, half), features.dtype)
-    moments, top, bottom = pl.pallas_call(
-        first_kernel,
-        out_shape=(jax.ShapeDtypeStruct((devices, 2, half), jnp.float32), edge, edge),
+    edges = 1 if tiles == 2 else 2
+    moments, *edge_rows = pl.pallas_call(
+        functools.partial(first_kernel, tiles == 2),
+        out_shape=(jax.ShapeDtypeStruct((devices, 2, half), jnp.float32),) + (edge,) * edges,
         in_specs=vmem_specs(1),
-        out_specs=tuple(vmem_specs(3)),
+        out_specs=tuple(vmem_specs(1 + edges)),
         compiler_params=params(),
+        cost_estimate=cost(1_000_000_000, 1_000_000),
         name="feature_moments",
     )(features)
     if tiles == 2:
-        facing = jnp.where(tile == 0, bottom, top)
-        up = down = lax.ppermute(facing, "tile", [(0, 1), (1, 0)])
+        (facing,) = edge_rows
         crossing = [
             (a * 2 + b, (a + 1) * 2 + 1 - b) for a in range(tms - 1) for b in range(2)
         ]
-        up_prev = down_prev = lax.ppermute(facing, grid_axes, crossing)
-        rims = [up, up_prev]
-        other_up, other_up_prev = (swap(rim) for rim in rims)
-        other_down, other_down_prev = other_up, other_up_prev
+        rims = [
+            lax.ppermute(facing, "tile", [(0, 1), (1, 0)]),
+            lax.ppermute(facing, grid_axes, crossing),
+        ]
     else:
-        up, down = shift(bottom, 0, 1), shift(top, 0, -1)
-        up_prev, down_prev = shift(bottom, 1, 1), shift(top, 1, -1)
-        other_up, other_down = swap(up), swap(down)
-        other_up_prev, other_down_prev = swap(up_prev), swap(down_prev)
+        top, bottom = edge_rows
+        rims = [
+            shift(bottom, 0, 1),
+            shift(bottom, 1, 1),
+            shift(top, 0, -1),
+            shift(top, 1, -1),
+        ]
+    other = swap(features)
     moments = to_everyone(moments)
-    other = swap(features)
+    previous, moments, *rims = lax.optimization_barrier((previous, moments, *rims))
     other_previous = swap(previous)
+    other_rims = [swap(rim) for rim in rims]
+    up, up_prev, down, down_prev = (rims * 2)[:4]
+    other_up, other_up_prev, other_down, other_down_prev = (other_rims * 2)[:4]
 
     hidden, moments_mid = pl.pallas_call(
         functools.partial(middle_kernel, tiles),

time: 56.6 us -> 47.6 us (0.84)
  blocking collectives: 21.7 us -> 8.9 us
  starting transfers between devices: 13.4 us -> 18.5 us
  local copies, waits for them, and re-layouts: 5.41 us -> 2.93 us
  Pallas kernels: 7.22 us -> 8.71 us
    all_to_all x2 -> x1, blocking collectives: 21.7 us -> 8.9 us  [to_everyone(): return lax.all_to_all(moments, AXES, 0, 0, tiled=True)]
    all_to_all x0 -> x1, waiting for transfers between devices: none -> 6.88 us  [to_everyone(): return lax.all_to_all(moments, AXES, 0, 0, tiled=True)]
    all_to_all x0 -> x1, starting transfers between devices: none -> 4.84 us  [to_everyone(): return lax.all_to_all(moments, AXES, 0, 0, tiled=True)]
    ppermute x2, waiting for transfers between devices: 4.51 us -> 0.01 us  [shift(): lax.ppermute(value, grid_axes, pairs_for(tms, tiles, tm_step, tile_step))]
    ppermute x2, waiting for transfers between devices: 3.76 us -> 0.01 us  [the longest x1 0.01 us: shards(): lax.ppermute(facing, grid_axes, crossing)]
    unnamed x24, local copies, waits for them, and re-layouts: 5.41 us -> 2.93 us
    ppermute x4, waiting for transfers between devices: 0.01 us -> 1.25 us  [swap(): return lax.ppermute(value, 'section', [(0, 1), (1, 0)])]
    pallas_call x1, Pallas kernels: 3.89 us -> 4.78 us  [shards(): pl.pallas_call(functools.partial(middle_kernel, tiles), out_shape=(jax.Sh...]
  transfers between devices with their start and end apart: 8 -> 9, of which waited for: 3 -> 2; matrix products, arithmetic and copies ran while one was open for 0% -> 0% of each run, Pallas kernels for 1% -> 2%
where the time goes in v4:
time: 47.6 us; the launch traced here: 47.3 us
  starting transfers between devices  18.5 us (39%)
  blocking collectives  8.9 us (19%)
  Pallas kernels  8.71 us (18%)
  waiting for transfers between devices  8.14 us (17%)
  local copies, waits for them, and re-layouts  2.93 us (6%)
    all_to_all x1, blocking collectives, to_everyone(): return lax.all_to_all(moments, AXES, 0, 0, tiled=True)  8.9 us
    ppermute x2, starting transfers between devices, shift(): lax.ppermute(value, grid_axes, pairs_for(tms, tiles, tm_step, tile_step))  7.55 us
    all_to_all x1, waiting for transfers between devices, to_everyone(): return lax.all_to_all(moments, AXES, 0, 0, tiled=True)  6.88 us
    all_to_all x1, starting transfers between devices, to_everyone(): return lax.all_to_all(moments, AXES, 0, 0, tiled=True)  4.84 us
    pallas_call x1, Pallas kernels, shards(): pl.pallas_call(functools.partial(middle_kernel, tiles), out_shape=(jax.Sh...  4.78 us
    ppermute x1, starting transfers between devices, shards(): lax.ppermute(facing, grid_axes, crossing)  4.53 us
    pallas_call x1, Pallas kernels, shards(): pl.pallas_call(functools.partial(last_kernel, tiles), out_shape=jax.Shape...  3.02 us
    unnamed x24, local copies, waits for them, and re-layouts  2.93 us
  transfers between devices with their start and end apart: 9, of which 2 were waited for; matrix products, arithmetic and copies ran while one was open for 0% of the time, Pallas kernels for 2%

profile of v4, /device:TPU:0, one launch (start us, length us, event | category | flops | bytes accessed | tf_op | source)
XLA Modules:
  0.0 47.3 jit_solution(7292866163973994775)
XLA Ops:
  0.0 0.0 copy-start
  0.0 5.0 %collective-permute-start = (bf16[2,8,64,128]{3,2,1,0:T(8,128)(2,1)}, bf16[2,8,64,128]{3,2,1,0:T(8,128)(2,1)S(1)}, u32[]{:S(2)}, u32[]{:S(2)}) collective-permute-start(bf16[2,8,64,128]{3,2,1,0:T(8,128)(2,1)} %x_ref.5), channel_id=1, source_target_pairs={{0,2},{1,3},{2,4},{3,5},{4,6},{5,7},{6,8},{7,9},{8,10},{9,11},{10,... | collective-permute-start | bytes 786440 | tf_op jit(solution)/shard_map/ppermute | solution.py:285
  5.0 0.0 copy-start.1
  5.0 0.9 %copy-done.1 = bf16[2,8,64,128]{3,2,1,0:T(8,128)(2,1)S(1)} copy-done((bf16[2,8,64,128]{3,2,1,0:T(8,128)(2,1)S(1)}, bf16[2,8,64,128]{3,2,1,0:T(8,128)(2,1)}, u32[]{:S(2)}) %copy-start.1) | copy-done | bytes 262168
  5.9 0.0 copy-start.2
  5.9 0.0 copy-start.5
  5.9 0.0 copy-start.6
  5.9 0.0 copy-start.7
  6.0 0.9 %feature_moments.1 = (f32[32,2,128]{2,1,0:T(2,128)}, bf16[2,2,64,128]{3,2,1,0:T(8,128)(2,1)}) custom-call(bf16[2,8,64,128]{3,2,1,0:T(8,128)(2,1)S(1)} %copy-done.1), custom_call_target="tpu_custom_call" | custom-call | flops 1000000000 | bytes 1000000 | tf_op jit(solution)/shard_map/feature_moments/pallas_call | solution.py:293
  6.8 0.0 copy-start.3
  6.9 0.0 copy-start.8
  6.9 4.5 %collective-permute-start.2 = (bf16[2,2,64,128]{3,2,1,0:T(8,128)(2,1)}, bf16[2,2,64,128]{3,2,1,0:T(8,128)(2,1)S(1)}, u32[]{:S(2)}, u32[]{:S(2)}) collective-permute-start(bf16[2,2,64,128]{3,2,1,0:T(8,128)(2,1)} %get-tuple-element.14), channel_id=1, source_target_pairs={{0,3},{1,2},{2,5},{3,4},{4,7},{5,6},{6,9},{7,8},{8,11},{9,10},{10,... | collective-permute-start | bytes 196616 | tf_op jit(solution)/shard_map/ppermute | solution.py:309
  11.4 0.6 %collective-permute-start.1 = (bf16[2,2,64,128]{3,2,1,0:T(8,128)(2,1)}, bf16[2,2,64,128]{3,2,1,0:T(8,128)(2,1)}, u32[]{:S(2)}, u32[]{:S(2)}) collective-permute-start(bf16[2,2,64,128]{3,2,1,0:T(8,128)(2,1)} %get-tuple-element.14), channel_id=1, source_target_pairs={{0,1},{1,0},{2,3},{3,2},{4,5},{5,4},{6,7},{7,6},{8,9},{9,8},{10,11... | collective-permute-start | bytes 196616 | tf_op jit(solution)/shard_map/ppermute | solution.py:308
  12.0 4.8 %all-to-all-start = ((f32[32,2,128]{2,1,0:T(2,128)}), f32[32,2,128]{2,1,0:T(2,128)S(1)}, u32[]{:S(2)}, u32[]{:S(2)}) async-start(f32[32,2,128]{2,1,0:T(2,128)} %get-tuple-element.13), calls=%async_computation | async-start | bytes 65536 | tf_op jit(solution)/shard_map/all_to_all | solution.py:259
  16.8 0.0 copy-done.2
  16.8 0.3 collective-permute-start.3
  17.1 6.9 %all-to-all-done.moments_ref = f32[32,2,128]{2,1,0:T(2,128)S(1)} async-done(((f32[32,2,128]{2,1,0:T(2,128)}), f32[32,2,128]{2,1,0:T(2,128)S(1)}, u32[]{:S(2)}, u32[]{:S(2)}) %all-to-all-start) | async-done | bytes 32800 | tf_op jit(solution)/shard_map/all_to_all | solution.py:259
  24.0 0.0 copy-start.4
  24.0 0.0 collective-permute-done.2.up_prev_ref.down_prev_ref
  24.0 0.0 collective-permute-done.1.up_ref.down_ref
  24.0 0.0 collective-permute-done.prev_ref
  24.0 0.1 collective-permute-start.4
  24.1 0.5 %collective-permute-start.5 = (bf16[2,2,64,128]{3,2,1,0:T(8,128)(2,1)}, bf16[2,2,64,128]{3,2,1,0:T(8,128)(2,1)S(1)}, u32[]{:S(2)}, u32[]{:S(2)}) collective-permute-start(bf16[2,2,64,128]{3,2,1,0:T(8,128)(2,1)} %collective-permute-done.1.up_ref.down_ref), channel_id=1, source_target_pairs={{0,16},{16,0},{1,17},{17,1},{2,18},{18,2},{3,19},{19,3},{4,20},{20... | collective-permute-start | bytes 196616 | tf_op jit(solution)/shard_map/ppermute | solution.py:288
  24.6 0.1 collective-permute-start.6
  24.7 0.0 collective-permute-done.3.other_x_ref
  24.7 1.2 %collective-permute-done.5.other_up_ref.other_down_ref = bf16[2,2,64,128]{3,2,1,0:T(8,128)(2,1)S(1)} collective-permute-done((bf16[2,2,64,128]{3,2,1,0:T(8,128)(2,1)}, bf16[2,2,64,128]{3,2,1,0:T(8,128)(2,1)S(1)}, u32[]{:S(2)}, u32[]{:S(2)}) %collective-permute-start.5) | collective-permute-done | bytes 65568 | tf_op jit(solution)/shard_map/ppermute | solution.py:288
  25.9 0.0 collective-permute-done.6.other_up_prev_ref.other_down_prev_ref
  25.9 0.0 collective-permute-done.4.other_prev_ref
  25.9 0.0 copy-done
  26.0 0.0 copy-done.5
  26.0 0.0 copy-done.6
  26.0 0.0 copy-done.7
  26.0 4.8 %norm_conv_in.1 = (bf16[2,10,48,128]{3,2,1,0:T(8,128)(2,1)S(1)}, f32[32,2,128]{2,1,0:T(2,128)S(1)}) custom-call(bf16[2,8,64,128]{3,2,1,0:T(8,128)(2,1)S(1)} %copy-done.2, bf16[2,8,64,128]{3,2,1,0:T(8,128)(2,1)S(1)} %collective-permute-done.prev_ref, bf16[2,2,64,128]{3,2,1,0:T(8,128)(2,1)} %collective-permute-done.1.up_ref.down_ref, ...), custom_call_target="tpu_custom_call" | custom-call | tf_op jit(solution)/shard_map/norm_conv_in/pallas_call | solution.py:327
  30.8 2.6 %collective-permute-start.7 = (bf16[2,10,48,128]{3,2,1,0:T(8,128)(2,1)S(1)}, bf16[2,10,48,128]{3,2,1,0:T(8,128)(2,1)S(1)}, u32[]{:S(2)}, u32[]{:S(2)}) collective-permute-start(bf16[2,10,48,128]{3,2,1,0:T(8,128)(2,1)S(1)} %get-tuple-element.19.hidden_ref), channel_id=1, source_target_pairs={{0,2},{1,3},{2,4},{3,5},{4,6},{5,7},{6,8},{7,9},{8,10},{9,11},{10,... | collective-permute-start | bytes 737288 | tf_op jit(solution)/shard_map/ppermute | solution.py:285
  33.4 8.9 %all_to_all.10.moments_ref = f32[32,2,128]{2,1,0:T(2,128)S(1)} all-to-all(f32[32,2,128]{2,1,0:T(2,128)S(1)} %get-tuple-element.20), channel_id=1, replica_groups=mesh['section'=2,'tm'=8,'tile'=2] {'section','tm','tile'}, dimensions={0} | all-to-all | bytes 65536 | tf_op jit(solution)/shard_map/all_to_all | solution.py:259
  42.3 0.0 collective-permute-done.7.before_ref
  42.3 0.0 copy-done.3
  42.3 0.0 copy-done.8
  42.3 0.0 copy-done.4
  42.3 0.0 copy-start.9
  42.3 0.6 %copy-done.9 = f32[128]{0:T(128)S(1)} copy-done((f32[128]{0:T(128)S(1)}, f32[128]{0:T(128)}, u32[]{:S(2)}) %copy-start.9) | copy-done | bytes 536
  42.9 0.0 copy-start.10
  42.9 0.7 %copy-done.10 = f32[128]{0:T(128)S(1)} copy-done((f32[128]{0:T(128)S(1)}, f32[128]{0:T(128)}, u32[]{:S(2)}) %copy-start.10) | copy-done | bytes 536
  43.6 0.0 copy-start.11
  43.6 0.7 %copy-done.11 = f32[128]{0:T(128)S(1)} copy-done((f32[128]{0:T(128)S(1)}, f32[128]{0:T(128)}, u32[]{:S(2)}) %copy-start.11) | copy-done | bytes 536
  44.3 3.0 %norm_conv_mid.1 = bf16[2,8,32,128]{3,2,1,0:T(8,128)(2,1)} custom-call(bf16[2,10,48,128]{3,2,1,0:T(8,128)(2,1)S(1)} %get-tuple-element.19.hidden_ref, bf16[2,10,48,128]{3,2,1,0:T(8,128)(2,1)S(1)} %collective-permute-done.7.before_ref, f32[32,2,128]{2,1,0:T(2,128)S(1)} %all_to_all.10.moments_ref, f32[1,128]{1,0:T(1,128)S(1)} %bitcast.10, ...), custom_call_target="tpu_custom_call" | custom-call | tf_op jit(solution)/shard_map/norm_conv_mid/pallas_call | solution.py:359
Async XLA Ops:
  0.0 26.0 %copy-start = (bf16[3,3,3,256,128]{4,3,2,1,0:T(8,128)(2,1)S(1)}, bf16[3,3,3,256,128]{4,3,2,1,0:T(8,128)(2,1)}, u32[]{:S(2)}) copy-start(bf16[3,3,3,256,128]{4,3,2,1,0:T(8,128)(2,1)} %weight_ref.2) | copy-start | bytes 5308420
  0.0 24.0 %collective-permute-start = (bf16[2,8,64,128]{3,2,1,0:T(8,128)(2,1)}, bf16[2,8,64,128]{3,2,1,0:T(8,128)(2,1)S(1)}, u32[]{:S(2)}, u32[]{:S(2)}) collective-permute-start(bf16[2,8,64,128]{3,2,1,0:T(8,128)(2,1)} %x_ref.5), channel_id=1, source_target_pairs={{0,2},{1,3},{2,4},{3,5},{4,6},{5,7},{6,8},{7,9},{8,10},{9,11},{10,... | collective-permute-start | bytes 786440 | tf_op jit(solution)/shard_map/ppermute | solution.py:285
  5.0 1.0 %copy-start.1 = (bf16[2,8,64,128]{3,2,1,0:T(8,128)(2,1)S(1)}, bf16[2,8,64,128]{3,2,1,0:T(8,128)(2,1)}, u32[]{:S(2)}) copy-start(bf16[2,8,64,128]{3,2,1,0:T(8,128)(2,1)} %x_ref.5) | copy-start | bytes 786436
  5.9 10.9 %copy-start.2 = (bf16[2,8,64,128]{3,2,1,0:T(8,128)(2,1)S(1)}, bf16[2,8,64,128]{3,2,1,0:T(8,128)(2,1)}, u32[]{:S(2)}) copy-start(bf16[2,8,64,128]{3,2,1,0:T(8,128)(2,1)} %x_ref.5) | copy-start | bytes 786436
  5.9 20.0 %copy-start.5 = (f32[256]{0:T(256)S(1)}, f32[256]{0:T(256)}, u32[]{:S(2)}) copy-start(f32[256]{0:T(256)} %param.12) | copy-start | bytes 3076
  5.9 20.0 %copy-start.6 = (f32[256]{0:T(256)S(1)}, f32[256]{0:T(256)}, u32[]{:S(2)}) copy-start(f32[256]{0:T(256)} %param.13) | copy-start | bytes 3076
  5.9 20.0 %copy-start.7 = (f32[128]{0:T(128)S(1)}, f32[128]{0:T(128)}, u32[]{:S(2)}) copy-start(f32[128]{0:T(128)} %param.15) | copy-start | bytes 1540
  6.8 35.4 %copy-start.3 = (bf16[3,3,3,128,128]{4,3,2,1,0:T(8,128)(2,1)S(1)}, bf16[3,3,3,128,128]{4,3,2,1,0:T(8,128)(2,1)}, u32[]{:S(2)}) copy-start(bf16[3,3,3,128,128]{4,3,2,1,0:T(8,128)(2,1)} %weight_ref.3) | copy-start | bytes 2654212
  6.9 35.4 %copy-start.8 = (f32[128]{0:T(128)S(1)}, f32[128]{0:T(128)}, u32[]{:S(2)}) copy-start(f32[128]{0:T(128)} %param.16) | copy-start | bytes 1540
  6.9 17.2 %collective-permute-start.2 = (bf16[2,2,64,128]{3,2,1,0:T(8,128)(2,1)}, bf16[2,2,64,128]{3,2,1,0:T(8,128)(2,1)S(1)}, u32[]{:S(2)}, u32[]{:S(2)}) collective-permute-start(bf16[2,2,64,128]{3,2,1,0:T(8,128)(2,1)} %get-tuple-element.14), channel_id=1, source_target_pairs={{0,3},{1,2},{2,5},{3,4},{4,7},{5,6},{6,9},{7,8},{8,11},{9,10},{10,... | collective-permute-start | bytes 196616 | tf_op jit(solution)/shard_map/ppermute | solution.py:309
  11.4 12.6 %collective-permute-start.1 = (bf16[2,2,64,128]{3,2,1,0:T(8,128)(2,1)}, bf16[2,2,64,128]{3,2,1,0:T(8,128)(2,1)}, u32[]{:S(2)}, u32[]{:S(2)}) collective-permute-start(bf16[2,2,64,128]{3,2,1,0:T(8,128)(2,1)} %get-tuple-element.14), channel_id=1, source_target_pairs={{0,1},{1,0},{2,3},{3,2},{4,5},{5,4},{6,7},{7,6},{8,9},{9,8},{10,11... | collective-permute-start | bytes 196616 | tf_op jit(solution)/shard_map/ppermute | solution.py:308
  12.0 12.1 %all-to-all-start = ((f32[32,2,128]{2,1,0:T(2,128)}), f32[32,2,128]{2,1,0:T(2,128)S(1)}, u32[]{:S(2)}, u32[]{:S(2)}) async-start(f32[32,2,128]{2,1,0:T(2,128)} %get-tuple-element.13), calls=%async_computation | async-start | bytes 65536 | tf_op jit(solution)/shard_map/all_to_all | solution.py:259
  16.8 7.9 %collective-permute-start.3 = (bf16[2,8,64,128]{3,2,1,0:T(8,128)(2,1)S(1)}, bf16[2,8,64,128]{3,2,1,0:T(8,128)(2,1)S(1)}, u32[]{:S(2)}, u32[]{:S(2)}) collective-permute-start(bf16[2,8,64,128]{3,2,1,0:T(8,128)(2,1)S(1)} %copy-done.2), channel_id=1, source_target_pairs={{0,16},{16,0},{1,17},{17,1},{2,18},{18,2},{3,19},{19,3},{4,20},{20... | collective-permute-start | bytes 786440 | tf_op jit(solution)/shard_map/ppermute | solution.py:288
  24.0 18.3 %copy-start.4 = (bf16[256,128]{1,0:T(8,128)(2,1)S(1)}, bf16[256,128]{1,0:T(8,128)(2,1)}, u32[]{:S(2)}) copy-start(bf16[256,128]{1,0:T(8,128)(2,1)} %skip_ref.1) | copy-start | bytes 196612
  24.0 1.9 %collective-permute-start.4 = (bf16[2,8,64,128]{3,2,1,0:T(8,128)(2,1)S(1)}, bf16[2,8,64,128]{3,2,1,0:T(8,128)(2,1)S(1)}, u32[]{:S(2)}, u32[]{:S(2)}) collective-permute-start(bf16[2,8,64,128]{3,2,1,0:T(8,128)(2,1)S(1)} %collective-permute-done.prev_ref), channel_id=1, source_target_pairs={{0,16},{16,0},{1,17},{17,1},{2,18},{18,2},{3,19},{19,3},{4,20},{20... | collective-permute-start | bytes 786440 | tf_op jit(solution)/shard_map/ppermute | solution.py:288
  24.1 1.8 %collective-permute-start.5 = (bf16[2,2,64,128]{3,2,1,0:T(8,128)(2,1)}, bf16[2,2,64,128]{3,2,1,0:T(8,128)(2,1)S(1)}, u32[]{:S(2)}, u32[]{:S(2)}) collective-permute-start(bf16[2,2,64,128]{3,2,1,0:T(8,128)(2,1)} %collective-permute-done.1.up_ref.down_ref), channel_id=1, source_target_pairs={{0,16},{16,0},{1,17},{17,1},{2,18},{18,2},{3,19},{19,3},{4,20},{20... | collective-permute-start | bytes 196616 | tf_op jit(solution)/shard_map/ppermute | solution.py:288
  24.6 1.3 %collective-permute-start.6 = (bf16[2,2,64,128]{3,2,1,0:T(8,128)(2,1)S(1)}, bf16[2,2,64,128]{3,2,1,0:T(8,128)(2,1)S(1)}, u32[]{:S(2)}, u32[]{:S(2)}) collective-permute-start(bf16[2,2,64,128]{3,2,1,0:T(8,128)(2,1)S(1)} %collective-permute-done.2.up_prev_ref.down_prev_ref), channel_id=1, source_target_pairs={{0,16},{16,0},{1,17},{17,1},{2,18},{18,2},{3,19},{19,3},{4,20},{20... | collective-permute-start | bytes 196616 | tf_op jit(solution)/shard_map/ppermute | solution.py:288
  30.8 11.5 %collective-permute-start.7 = (bf16[2,10,48,128]{3,2,1,0:T(8,128)(2,1)S(1)}, bf16[2,10,48,128]{3,2,1,0:T(8,128)(2,1)S(1)}, u32[]{:S(2)}, u32[]{:S(2)}) collective-permute-start(bf16[2,10,48,128]{3,2,1,0:T(8,128)(2,1)S(1)} %get-tuple-element.19.hidden_ref), channel_id=1, source_target_pairs={{0,2},{1,3},{2,4},{3,5},{4,6},{5,7},{6,8},{7,9},{8,10},{9,11},{10,... | collective-permute-start | bytes 737288 | tf_op jit(solution)/shard_map/ppermute | solution.py:285
  42.3 0.7 %copy-start.9 = (f32[128]{0:T(128)S(1)}, f32[128]{0:T(128)}, u32[]{:S(2)}) copy-start(f32[128]{0:T(128)} %param.17) | copy-start | bytes 1540
  42.9 0.7 %copy-start.10 = (f32[128]{0:T(128)S(1)}, f32[128]{0:T(128)}, u32[]{:S(2)}) copy-start(f32[128]{0:T(128)} %param.19) | copy-start | bytes 1540
  43.6 0.7 %copy-start.11 = (f32[128]{0:T(128)S(1)}, f32[128]{0:T(128)}, u32[]{:S(2)}) copy-start(f32[128]{0:T(128)} %param.21) | copy-start | bytes 1540

commit v5 on v4

--- a/solution.py
+++ b/solution.py
@@ -50,14 +50,19 @@
     )[:1]
 
 
-def scale_and_offset(moments, cells, width, gain, shift):
-    devices, _, channels = moments.shape
+def scale_and_offset(refs, cells, width, gain, shift):
+    channels = refs[0].shape[-1]
+    devices = sum(ref.shape[0] for ref in refs)
     matrix = group_matrix(channels, width)
-    means = moments[:, 0, :]
-    spreads = moments[:, 1, :]
-    mean = group_sum(jnp.sum(means, axis=0, keepdims=True), matrix) * (1.0 / (devices * width))
-    off = means - mean
-    total = jnp.sum(spreads + float(cells) * (off * off), axis=0, keepdims=True)
+    moments = [ref[...] for ref in refs]
+    summed = sum(jnp.sum(part[:, 0, :], axis=0, keepdims=True) for part in moments)
+    mean = group_sum(summed, matrix) * (1.0 / (devices * width))
+    total = 0.0
+    for part in moments:
+        off = part[:, 0, :] - mean
+        total = total + jnp.sum(
+            part[:, 1, :] + float(cells) * (off * off), axis=0, keepdims=True
+        )
     spread = group_sum(total, matrix) * (1.0 / (cells * devices * width))
     scale = lax.rsqrt(spread + 1e-6) * gain
     return mean, scale, shift
@@ -114,11 +119,13 @@
     other_up_prev_ref,
     other_down_prev_ref,
     moments_ref,
+    other_moments_ref,
     gain_ref,
     shift_ref,
     weight_ref,
     bias_ref,
     hidden_ref,
+    sent_ref,
     out_moments_ref,
     act_ref,
 ):
@@ -127,23 +134,24 @@
     width = columns // 2 + RIM
     first = pl.multiple_of(section * (columns - width), RIM)
     cols = pl.ds(first, width)
-    per_section = moments_ref.shape[0] // 2
     pieces = (
         (
             section,
+            moments_ref,
             ((x_ref, up_ref, down_ref), (prev_ref, up_prev_ref, down_prev_ref)),
         ),
         (
             1 - section,
+            other_moments_ref,
             (
                 (other_x_ref, other_up_ref, other_down_ref),
                 (other_prev_ref, other_up_prev_ref, other_down_prev_ref),
             ),
         ),
     )
-    for which, (now, before) in pieces:
+    for which, moments, (now, before) in pieces:
         norm = scale_and_offset(
-            moments_ref[pl.ds(which * per_section, per_section)],
+            [moments],
             frames * rows * columns,
             2 * half // GROUPS,
             gain_ref[pl.ds(which, 1), :],
@@ -171,14 +179,24 @@
         for f in range(frames):
             act_ref[f] = act_ref[frames]
 
+    own = columns // 2
+    sent_rows = sent_ref.shape[1] - 1
+    top = sent_start(tiles, tile)
     for f in range(frames):
         hidden = conv_rows(act_ref, weight_ref, f, rows + 2, width) + bias_ref[...]
         hidden_ref[f] = hidden.astype(jnp.bfloat16)
-
-    cells = hidden_ref[:, 1 : 1 + rows, pl.ds(first, columns // 2), :]
+        sent_ref[f, :sent_rows] = hidden_ref[f, pl.ds(top, sent_rows), pl.ds(first, own), :]
+        rim = jnp.where(section == 0, hidden[:, own, :], hidden[:, width - own - 1, :])
+        spare = jnp.zeros((own - rim.shape[0], rim.shape[1]), jnp.float32)
+        sent_ref[f, sent_rows] = jnp.concatenate([rim, spare], axis=0).astype(jnp.bfloat16)
+
+    cells = hidden_ref[:, 1 : 1 + rows, pl.ds(first, own), :]
     cells = cells.astype(jnp.float32).reshape(-1, cells.shape[-1])
-    own = moments_of(cells)
-    out_moments_ref[...] = jnp.broadcast_to(own[None], out_moments_ref.shape)
+    out_moments_ref[...] = jnp.broadcast_to(moments_of(cells)[None], out_moments_ref.shape)
+
+
+def sent_start(tiles, tile):
+    return 1 - tile if tiles == 2 else 0
 
 
 def last_kernel(
@@ -186,6 +204,7 @@
     hidden_ref,
     before_ref,
     moments_ref,
+    other_moments_ref,
     gain_ref,
     shift_ref,
     weight_ref,
@@ -203,16 +222,25 @@
     columns = x_ref.shape[2]
     half = x_ref.shape[3]
     own = columns // 2
+    sent_rows = before_ref.shape[1] - 1
+    top = sent_start(tiles, tile)
+    first = pl.multiple_of(section * (width - own), RIM)
+    beside = pl.multiple_of((1 - section) * own, RIM)
     norm = scale_and_offset(
-        moments_ref[...],
+        [moments_ref, other_moments_ref],
         frames * rows * own,
         outputs // GROUPS,
         gain_ref[...],
         shift_ref[...],
     )
     for f in range(frames):
-        act_ref[f] = apply_norm(before_ref[f], norm)
         act_ref[frames + f] = apply_norm(hidden_ref[f], norm)
+        act_ref[f, pl.ds(top, sent_rows), pl.ds(first, own), :] = apply_norm(
+            before_ref[f, :sent_rows], norm
+        )
+        rim = apply_norm(before_ref[f, sent_rows], norm).astype(jnp.float32)[:padded]
+        rim = jnp.broadcast_to(rim[:, None, :], (padded, width - own, outputs))
+        act_ref[f, :, pl.ds(beside, width - own), :] = rim.astype(jnp.bfloat16)
 
     @pl.when(tile == 0)
     def _():
@@ -256,7 +284,7 @@
 
 
 def to_everyone(moments):
-    return lax.all_to_all(moments, AXES, 0, 0, tiled=True)
+    return lax.all_to_all(moments, ("tm", "tile"), 0, 0, tiled=True)
 
 
 def shards(
@@ -273,7 +301,7 @@
     skip_bias,
 ):
     sections, tms, tiles = (lax.axis_size(axis) for axis in AXES)
-    devices = sections * tms * tiles
+    parties = tms * tiles
     frames, rows, columns, half = features.shape
     own = columns // sections
     width = own + RIM
@@ -292,7 +320,7 @@
     edges = 1 if tiles == 2 else 2
     moments, *edge_rows = pl.pallas_call(
         functools.partial(first_kernel, tiles == 2),
-        out_shape=(jax.ShapeDtypeStruct((devices, 2, half), jnp.float32),) + (edge,) * edges,
+        out_shape=(jax.ShapeDtypeStruct((parties, 2, half), jnp.float32),) + (edge,) * edges,
         in_specs=vmem_specs(1),
         out_specs=tuple(vmem_specs(1 + edges)),
         compiler_params=params(),
@@ -319,21 +347,25 @@
     other = swap(features)
     moments = to_everyone(moments)
     previous, moments, *rims = lax.optimization_barrier((previous, moments, *rims))
+    other_moments = swap(moments)
     other_previous = swap(previous)
     other_rims = [swap(rim) for rim in rims]
     up, up_prev, down, down_prev = (rims * 2)[:4]
     other_up, other_up_prev, other_down, other_down_prev = (other_rims * 2)[:4]
 
-    hidden, moments_mid = pl.pallas_call(
+    sent_rows = rows + (1 if tiles == 2 else 2)
+    hidden, sent, moments_mid = pl.pallas_call(
         functools.partial(middle_kernel, tiles),
         out_shape=(
             jax.ShapeDtypeStruct((frames, rows + 2, width, middle), jnp.bfloat16),
-            jax.ShapeDtypeStruct((devices, 2, middle), jnp.float32),
+            jax.ShapeDtypeStruct((frames, sent_rows + 1, own, middle), jnp.bfloat16),
+            jax.ShapeDtypeStruct((parties, 2, middle), jnp.float32),
         ),
-        in_specs=vmem_specs(17),
-        out_specs=tuple(vmem_specs(2)),
+        in_specs=vmem_specs(18),
+        out_specs=tuple(vmem_specs(3)),
         scratch_shapes=[pltpu.VMEM((2 * frames, rows + 4, width, 2 * half), jnp.bfloat16)],
         compiler_params=params(),
+        cost_estimate=cost(4_000_000_000, 1_000_000),
         name="norm_conv_in",
     )(
         features,
@@ -349,17 +381,18 @@
         other_up_prev,
         other_down_prev,
         moments,
+        other_moments,
         norm_gain_in.reshape(2, half),
         norm_shift_in.reshape(2, half),
         conv_in_weight,
         conv_in_bias.reshape(1, middle),
     )
-    before = shift(hidden, 1, 0)
+    before = shift(sent, 1, 0)
     moments_mid = to_everyone(moments_mid)
     return pl.pallas_call(
         functools.partial(last_kernel, tiles),
         out_shape=jax.ShapeDtypeStruct((frames, rows, own, outputs), jnp.bfloat16),
-        in_specs=vmem_specs(11),
+        in_specs=vmem_specs(12),
         out_specs=pl.BlockSpec(memory_space=pltpu.VMEM),
         scratch_shapes=[pltpu.VMEM((2 * frames, rows + 2, width, middle), jnp.bfloat16)],
         compiler_params=params(),
@@ -368,6 +401,7 @@
         hidden,
         before,
         moments_mid,
+        swap(moments_mid),
         norm_gain_mid.reshape(1, middle),
         norm_shift_mid.reshape(1, middle),
         conv_mid_weight,

time: 47.6 us -> 47.9 us (level)
  local copies, waits for them, and re-layouts: 2.93 us -> 1 us
  waiting for transfers between devices: 8.14 us -> 9.28 us
  blocking collectives: 8.9 us -> 10 us
  Pallas kernels: 8.71 us -> 7.78 us
  starting transfers between devices: 18.5 us -> 19.3 us
    unnamed x24, local copies, waits for them, and re-layouts: 2.93 us -> 1 us
    all_to_all x1, blocking collectives: 8.9 us -> 10 us  [to_everyone(): return lax.all_to_all(moments, ('tm', 'tile'), 0, 0, tiled=True)]
    all_to_all x1, starting transfers between devices: 4.84 us -> 5.85 us  [to_everyone(): return lax.all_to_all(moments, ('tm', 'tile'), 0, 0, tiled=True)]
    pallas_call x1, Pallas kernels: 4.78 us -> 3.88 us  [shards(): pl.pallas_call(functools.partial(middle_kernel, tiles), out_shape=(jax.Sh...]
    ppermute x4 -> x6, waiting for transfers between devices: 1.25 us -> 2.03 us  [swap(): return lax.ppermute(value, 'section', [(0, 1), (1, 0)])]
    ppermute x4 -> x6, starting transfers between devices: 0.96 us -> 1.15 us  [swap(): return lax.ppermute(value, 'section', [(0, 1), (1, 0)])]
  transfers between devices with their start and end apart: 9 -> 11, of which waited for: 2 -> 3; matrix products, arithmetic and copies ran while one was open for 0% -> 0% of each run, Pallas kernels for 2% -> 2%
where the time goes in v5:
time: 47.9 us; the launch traced here: 47.6 us
  starting transfers between devices  19.3 us (40%)
  blocking collectives  10 us (21%)
  waiting for transfers between devices  9.28 us (19%)
  Pallas kernels  7.78 us (16%)
  local copies, waits for them, and re-layouts  1 us (2%)
    all_to_all x1, blocking collectives, to_everyone(): return lax.all_to_all(moments, ('tm', 'tile'), 0, 0, tiled=True)  10 us
    ppermute x2, starting transfers between devices, shift(): lax.ppermute(value, grid_axes, pairs_for(tms, tiles, tm_step, tile_step))  7.31 us
    all_to_all x1, waiting for transfers between devices, to_everyone(): return lax.all_to_all(moments, ('tm', 'tile'), 0, 0, tiled=True)  7.24 us
    all_to_all x1, starting transfers between devices, to_everyone(): return lax.all_to_all(moments, ('tm', 'tile'), 0, 0, tiled=True)  5.85 us
    ppermute x1, starting transfers between devices, shards(): lax.ppermute(facing, grid_axes, crossing)  4.4 us
    pallas_call x1, Pallas kernels, shards(): pl.pallas_call(functools.partial(middle_kernel, tiles), out_shape=(jax.Sh...  3.88 us
    pallas_call x1, Pallas kernels, shards(): pl.pallas_call(functools.partial(last_kernel, tiles), out_shape=jax.Shape...  3.01 us
    ppermute x6, waiting for transfers between devices, swap(): return lax.ppermute(value, 'section', [(0, 1), (1, 0)])  2.03 us
  transfers between devices with their start and end apart: 11, of which 3 were waited for; matrix products, arithmetic and copies ran while one was open for 0% of the time, Pallas kernels for 2%

profile of v5, /device:TPU:0, one launch (start us, length us, event | category | flops | bytes accessed | tf_op | source)
XLA Modules:
  0.0 47.6 jit_solution(1052546402016121601)
XLA Ops:
  0.0 4.8 %collective-permute-start = (bf16[2,8,64,128]{3,2,1,0:T(8,128)(2,1)}, bf16[2,8,64,128]{3,2,1,0:T(8,128)(2,1)S(1)}, u32[]{:S(2)}, u32[]{:S(2)}) collective-permute-start(bf16[2,8,64,128]{3,2,1,0:T(8,128)(2,1)} %x_ref.5), channel_id=1, source_target_pairs={{0,2},{1,3},{2,4},{3,5},{4,6},{5,7},{6,8},{7,9},{8,10},{9,11},{10,... | collective-permute-start | bytes 786440 | tf_op jit(solution)/shard_map/ppermute | solution.py:313
  4.9 0.0 copy-start.1
  4.9 0.9 %copy-done.1 = bf16[2,8,64,128]{3,2,1,0:T(8,128)(2,1)S(1)} copy-done((bf16[2,8,64,128]{3,2,1,0:T(8,128)(2,1)S(1)}, bf16[2,8,64,128]{3,2,1,0:T(8,128)(2,1)}, u32[]{:S(2)}) %copy-start.1) | copy-done | bytes 262168
  5.8 0.0 copy-start.2
  5.8 0.0 copy-start.8
  5.8 0.0 copy-start.11
  5.8 0.9 %feature_moments.1 = (f32[16,2,128]{2,1,0:T(2,128)}, bf16[2,2,64,128]{3,2,1,0:T(8,128)(2,1)S(1)}) custom-call(bf16[2,8,64,128]{3,2,1,0:T(8,128)(2,1)S(1)} %copy-done.1), custom_call_target="tpu_custom_call" | custom-call | flops 1000000000 | bytes 1000000 | tf_op jit(solution)/shard_map/feature_moments/pallas_call | solution.py:321
  6.7 4.4 %collective-permute-start.2 = (bf16[2,2,64,128]{3,2,1,0:T(8,128)(2,1)S(1)}, bf16[2,2,64,128]{3,2,1,0:T(8,128)(2,1)S(1)}, u32[]{:S(2)}, u32[]{:S(2)}) collective-permute-start(bf16[2,2,64,128]{3,2,1,0:T(8,128)(2,1)S(1)} %get-tuple-element.15), channel_id=1, source_target_pairs={{0,3},{1,2},{2,5},{3,4},{4,7},{5,6},{6,9},{7,8},{8,11},{9,10},{10,... | collective-permute-start | bytes 196616 | tf_op jit(solution)/shard_map/ppermute | solution.py:337
  11.1 0.6 %collective-permute-start.1 = (bf16[2,2,64,128]{3,2,1,0:T(8,128)(2,1)S(1)}, bf16[2,2,64,128]{3,2,1,0:T(8,128)(2,1)S(1)}, u32[]{:S(2)}, u32[]{:S(2)}) collective-permute-start(bf16[2,2,64,128]{3,2,1,0:T(8,128)(2,1)S(1)} %get-tuple-element.15), channel_id=1, source_target_pairs={{0,1},{1,0},{2,3},{3,2},{4,5},{5,4},{6,7},{7,6},{8,9},{9,8},{10,11... | collective-permute-start | bytes 196616 | tf_op jit(solution)/shard_map/ppermute | solution.py:336
  11.7 5.9 %all-to-all-start = ((f32[16,2,128]{2,1,0:T(2,128)}), f32[16,2,128]{2,1,0:T(2,128)S(1)}, u32[]{:S(2)}, u32[]{:S(2)}) async-start(f32[16,2,128]{2,1,0:T(2,128)} %get-tuple-element.14), calls=%async_computation | async-start | bytes 32768 | tf_op jit(solution)/shard_map/all_to_all | solution.py:287
  17.6 0.0 copy-done.2
  17.6 0.1 collective-permute-start.3
  17.7 7.2 %all-to-all-done.moments_ref = f32[16,2,128]{2,1,0:T(2,128)S(1)} async-done(((f32[16,2,128]{2,1,0:T(2,128)}), f32[16,2,128]{2,1,0:T(2,128)S(1)}, u32[]{:S(2)}, u32[]{:S(2)}) %all-to-all-start) | async-done | bytes 16416 | tf_op jit(solution)/shard_map/all_to_all | solution.py:287
  24.9 0.0 collective-permute-done.2.up_prev_ref.down_prev_ref
  24.9 0.0 collective-permute-done.1.up_ref.down_ref
  24.9 0.0 collective-permute-done.prev_ref
  24.9 0.1 collective-permute-start.4
  25.0 0.5 %collective-permute-start.5 = (bf16[2,2,64,128]{3,2,1,0:T(8,128)(2,1)S(1)}, bf16[2,2,64,128]{3,2,1,0:T(8,128)(2,1)S(1)}, u32[]{:S(2)}, u32[]{:S(2)}) collective-permute-start(bf16[2,2,64,128]{3,2,1,0:T(8,128)(2,1)S(1)} %collective-permute-done.1.up_ref.down_ref), channel_id=1, source_target_pairs={{0,16},{16,0},{1,17},{17,1},{2,18},{18,2},{3,19},{19,3},{4,20},{20... | collective-permute-start | bytes 196616 | tf_op jit(solution)/shard_map/ppermute | solution.py:316
  25.5 0.1 collective-permute-start.6
  25.6 0.4 collective-permute-start.7
  26.0 0.0 collective-permute-done.3.other_x_ref
  26.0 0.8 %collective-permute-done.7.other_moments_ref = f32[16,2,128]{2,1,0:T(2,128)S(1)} collective-permute-done((f32[16,2,128]{2,1,0:T(2,128)S(1)}, f32[16,2,128]{2,1,0:T(2,128)S(1)}, u32[]{:S(2)}, u32[]{:S(2)}) %collective-permute-start.7) | collective-permute-done | bytes 16416 | tf_op jit(solution)/shard_map/ppermute | solution.py:316
  26.8 0.0 collective-permute-done.5.other_up_ref.other_down_ref
  26.8 0.0 collective-permute-done.6.other_up_prev_ref.other_down_prev_ref
  26.8 0.0 collective-permute-done.4.other_prev_ref
  26.8 0.0 copy-done.8
  26.9 0.0 copy-done.9
  26.9 0.0 copy-done.10
  26.9 0.0 copy-done.11
  26.9 0.0 copy-start
  26.9 0.0 copy-start.3
  26.9 0.0 copy-start.4
  26.9 0.0 copy-start.5
  26.9 0.0 copy-start.6
  26.9 0.0 copy-start.7
  27.0 3.9 %norm_conv_in.1 = (bf16[2,10,48,128]{3,2,1,0:T(8,128)(2,1)S(1)}, bf16[2,10,32,128]{3,2,1,0:T(8,128)(2,1)S(1)}, f32[16,2,128]{2,1,0:T(2,128)S(1)}) custom-call(bf16[2,8,64,128]{3,2,1,0:T(8,128)(2,1)S(1)} %copy-done.2, bf16[2,8,64,128]{3,2,1,0:T(8,128)(2,1)S(1)} %collective-permute-done.prev_ref, ...), custom_call_target="tpu_custom_call" | custom-call | flops 4000000000 | bytes 1000000 | tf_op jit(solution)/shard_map/norm_conv_in/pallas_call | solution.py:357
  30.8 2.5 %collective-permute-start.8 = (bf16[2,10,32,128]{3,2,1,0:T(8,128)(2,1)S(1)}, bf16[2,10,32,128]{3,2,1,0:T(8,128)(2,1)S(1)}, u32[]{:S(2)}, u32[]{:S(2)}) collective-permute-start(bf16[2,10,32,128]{3,2,1,0:T(8,128)(2,1)S(1)} %get-tuple-element.21), channel_id=1, source_target_pairs={{0,2},{1,3},{2,4},{3,5},{4,6},{5,7},{6,8},{7,9},{8,10},{9,11},{10,... | collective-permute-start | bytes 491528 | tf_op jit(solution)/shard_map/ppermute | solution.py:313
  33.3 10.0 %all_to_all.10.moments_ref = f32[16,2,128]{2,1,0:T(2,128)S(1)} all-to-all(f32[16,2,128]{2,1,0:T(2,128)S(1)} %get-tuple-element.22), channel_id=1, replica_groups=mesh['section'=2,'tm'=8,'tile'=2] {'tm','tile'}, dimensions={0} | all-to-all | bytes 32768 | tf_op jit(solution)/shard_map/all_to_all | solution.py:287
  43.3 0.0 collective-permute-start.9
  43.4 1.2 %collective-permute-done.9.other_moments_ref = f32[16,2,128]{2,1,0:T(2,128)S(1)} collective-permute-done((f32[16,2,128]{2,1,0:T(2,128)S(1)}, f32[16,2,128]{2,1,0:T(2,128)S(1)}, u32[]{:S(2)}, u32[]{:S(2)}) %collective-permute-start.9) | collective-permute-done | bytes 16416 | tf_op jit(solution)/shard_map/ppermute | solution.py:316
  44.5 0.0 collective-permute-done.8.before_ref
  44.5 0.0 copy-done
  44.5 0.0 copy-done.3
  44.5 0.0 copy-done.4
  44.6 0.0 copy-done.5
  44.6 0.0 copy-done.6
  44.6 0.0 copy-done.7
  44.6 3.0 %norm_conv_mid.1 = bf16[2,8,32,128]{3,2,1,0:T(8,128)(2,1)} custom-call(bf16[2,10,48,128]{3,2,1,0:T(8,128)(2,1)S(1)} %get-tuple-element.20.hidden_ref, bf16[2,10,32,128]{3,2,1,0:T(8,128)(2,1)S(1)} %collective-permute-done.8.before_ref, f32[16,2,128]{2,1,0:T(2,128)S(1)} %all_to_all.10.moments_ref, f32[16,2,128]{2,1,0:T(2,128)S(1)} %collective-permute-done.9.other_moments_ref, ...), custom_call_target="tpu_custom_call" | custom-call | tf_op jit(solution)/shard_map/norm_conv_mid/pallas_call | solution.py:392
  (2 shorter events, 0.0 us)
Async XLA Ops:
  0.0 24.9 %collective-permute-start = (bf16[2,8,64,128]{3,2,1,0:T(8,128)(2,1)}, bf16[2,8,64,128]{3,2,1,0:T(8,128)(2,1)S(1)}, u32[]{:S(2)}, u32[]{:S(2)}) collective-permute-start(bf16[2,8,64,128]{3,2,1,0:T(8,128)(2,1)} %x_ref.5), channel_id=1, source_target_pairs={{0,2},{1,3},{2,4},{3,5},{4,6},{5,7},{6,8},{7,9},{8,10},{9,11},{10,... | collective-permute-start | bytes 786440 | tf_op jit(solution)/shard_map/ppermute | solution.py:313
  4.9 1.0 %copy-start.1 = (bf16[2,8,64,128]{3,2,1,0:T(8,128)(2,1)S(1)}, bf16[2,8,64,128]{3,2,1,0:T(8,128)(2,1)}, u32[]{:S(2)}) copy-start(bf16[2,8,64,128]{3,2,1,0:T(8,128)(2,1)} %x_ref.5) | copy-start | bytes 786436
  5.8 11.8 %copy-start.2 = (bf16[2,8,64,128]{3,2,1,0:T(8,128)(2,1)S(1)}, bf16[2,8,64,128]{3,2,1,0:T(8,128)(2,1)}, u32[]{:S(2)}) copy-start(bf16[2,8,64,128]{3,2,1,0:T(8,128)(2,1)} %x_ref.5) | copy-start | bytes 786436
  5.8 21.0 %copy-start.8 = (bf16[3,3,3,256,128]{4,3,2,1,0:T(8,128)(2,1)S(1)}, bf16[3,3,3,256,128]{4,3,2,1,0:T(8,128)(2,1)}, u32[]{:S(2)}) copy-start(bf16[3,3,3,256,128]{4,3,2,1,0:T(8,128)(2,1)} %weight_ref.2) | copy-start | bytes 5308420
  5.8 21.0 %copy-start.9 = (f32[256]{0:T(256)S(1)}, f32[256]{0:T(256)}, u32[]{:S(2)}) copy-start(f32[256]{0:T(256)} %param.12) | copy-start | bytes 3076
  5.8 21.1 %copy-start.10 = (f32[256]{0:T(256)S(1)}, f32[256]{0:T(256)}, u32[]{:S(2)}) copy-start(f32[256]{0:T(256)} %param.13) | copy-start | bytes 3076
  5.8 21.1 %copy-start.11 = (f32[128]{0:T(128)S(1)}, f32[128]{0:T(128)}, u32[]{:S(2)}) copy-start(f32[128]{0:T(128)} %param.15) | copy-start | bytes 1540
  6.7 18.2 %collective-permute-start.2 = (bf16[2,2,64,128]{3,2,1,0:T(8,128)(2,1)S(1)}, bf16[2,2,64,128]{3,2,1,0:T(8,128)(2,1)S(1)}, u32[]{:S(2)}, u32[]{:S(2)}) collective-permute-start(bf16[2,2,64,128]{3,2,1,0:T(8,128)(2,1)S(1)} %get-tuple-element.15), channel_id=1, source_target_pairs={{0,3},{1,2},{2,5},{3,4},{4,7},{5,6},{6,9},{7,8},{8,11},{9,10},{10,... | collective-permute-start | bytes 196616 | tf_op jit(solution)/shard_map/ppermute | solution.py:337
  11.1 13.8 %collective-permute-start.1 = (bf16[2,2,64,128]{3,2,1,0:T(8,128)(2,1)S(1)}, bf16[2,2,64,128]{3,2,1,0:T(8,128)(2,1)S(1)}, u32[]{:S(2)}, u32[]{:S(2)}) collective-permute-start(bf16[2,2,64,128]{3,2,1,0:T(8,128)(2,1)S(1)} %get-tuple-element.15), channel_id=1, source_target_pairs={{0,1},{1,0},{2,3},{3,2},{4,5},{5,4},{6,7},{7,6},{8,9},{9,8},{10,11... | collective-permute-start | bytes 196616 | tf_op jit(solution)/shard_map/ppermute | solution.py:336
  11.7 13.2 %all-to-all-start = ((f32[16,2,128]{2,1,0:T(2,128)}), f32[16,2,128]{2,1,0:T(2,128)S(1)}, u32[]{:S(2)}, u32[]{:S(2)}) async-start(f32[16,2,128]{2,1,0:T(2,128)} %get-tuple-element.14), calls=%async_computation | async-start | bytes 32768 | tf_op jit(solution)/shard_map/all_to_all | solution.py:287
  17.6 8.4 %collective-permute-start.3 = (bf16[2,8,64,128]{3,2,1,0:T(8,128)(2,1)S(1)}, bf16[2,8,64,128]{3,2,1,0:T(8,128)(2,1)S(1)}, u32[]{:S(2)}, u32[]{:S(2)}) collective-permute-start(bf16[2,8,64,128]{3,2,1,0:T(8,128)(2,1)S(1)} %copy-done.2), channel_id=1, source_target_pairs={{0,16},{16,0},{1,17},{17,1},{2,18},{18,2},{3,19},{19,3},{4,20},{20... | collective-permute-start | bytes 786440 | tf_op jit(solution)/shard_map/ppermute | solution.py:316
  24.9 1.9 %collective-permute-start.4 = (bf16[2,8,64,128]{3,2,1,0:T(8,128)(2,1)S(1)}, bf16[2,8,64,128]{3,2,1,0:T(8,128)(2,1)S(1)}, u32[]{:S(2)}, u32[]{:S(2)}) collective-permute-start(bf16[2,8,64,128]{3,2,1,0:T(8,128)(2,1)S(1)} %collective-permute-done.prev_ref), channel_id=1, source_target_pairs={{0,16},{16,0},{1,17},{17,1},{2,18},{18,2},{3,19},{19,3},{4,20},{20... | collective-permute-start | bytes 786440 | tf_op jit(solution)/shard_map/ppermute | solution.py:316
  25.0 1.9 %collective-permute-start.5 = (bf16[2,2,64,128]{3,2,1,0:T(8,128)(2,1)S(1)}, bf16[2,2,64,128]{3,2,1,0:T(8,128)(2,1)S(1)}, u32[]{:S(2)}, u32[]{:S(2)}) collective-permute-start(bf16[2,2,64,128]{3,2,1,0:T(8,128)(2,1)S(1)} %collective-permute-done.1.up_ref.down_ref), channel_id=1, source_target_pairs={{0,16},{16,0},{1,17},{17,1},{2,18},{18,2},{3,19},{19,3},{4,20},{20... | collective-permute-start | bytes 196616 | tf_op jit(solution)/shard_map/ppermute | solution.py:316
  25.5 1.4 %collective-permute-start.6 = (bf16[2,2,64,128]{3,2,1,0:T(8,128)(2,1)S(1)}, bf16[2,2,64,128]{3,2,1,0:T(8,128)(2,1)S(1)}, u32[]{:S(2)}, u32[]{:S(2)}) collective-permute-start(bf16[2,2,64,128]{3,2,1,0:T(8,128)(2,1)S(1)} %collective-permute-done.2.up_prev_ref.down_prev_ref), channel_id=1, source_target_pairs={{0,16},{16,0},{1,17},{17,1},{2,18},{18,2},{3,19},{19,3},{4,20},{20... | collective-permute-start | bytes 196616 | tf_op jit(solution)/shard_map/ppermute | solution.py:316
  25.6 1.3 %collective-permute-start.7 = (f32[16,2,128]{2,1,0:T(2,128)S(1)}, f32[16,2,128]{2,1,0:T(2,128)S(1)}, u32[]{:S(2)}, u32[]{:S(2)}) collective-permute-start(f32[16,2,128]{2,1,0:T(2,128)S(1)} %all-to-all-done.moments_ref), channel_id=1, source_target_pairs={{0,16},{16,0},{1,17},{17,1},{2,18},{18,2},{3,19},{19,3},{4,20},{20... | collective-permute-start | bytes 49160 | tf_op jit(solution)/shard_map/ppermute | solution.py:316
  26.9 17.7 %copy-start = (bf16[3,3,3,128,128]{4,3,2,1,0:T(8,128)(2,1)S(1)}, bf16[3,3,3,128,128]{4,3,2,1,0:T(8,128)(2,1)}, u32[]{:S(2)}) copy-start(bf16[3,3,3,128,128]{4,3,2,1,0:T(8,128)(2,1)} %weight_ref.3) | copy-start | bytes 2654212
  26.9 17.6 %copy-start.3 = (bf16[256,128]{1,0:T(8,128)(2,1)S(1)}, bf16[256,128]{1,0:T(8,128)(2,1)}, u32[]{:S(2)}) copy-start(bf16[256,128]{1,0:T(8,128)(2,1)} %skip_ref.1) | copy-start | bytes 196612
  26.9 17.6 %copy-start.4 = (f32[128]{0:T(128)S(1)}, f32[128]{0:T(128)}, u32[]{:S(2)}) copy-start(f32[128]{0:T(128)} %param.16) | copy-start | bytes 1540
  26.9 17.6 %copy-start.5 = (f32[128]{0:T(128)S(1)}, f32[128]{0:T(128)}, u32[]{:S(2)}) copy-start(f32[128]{0:T(128)} %param.17) | copy-start | bytes 1540
  26.9 17.6 %copy-start.6 = (f32[128]{0:T(128)S(1)}, f32[128]{0:T(128)}, u32[]{:S(2)}) copy-start(f32[128]{0:T(128)} %param.19) | copy-start | bytes 1540
  26.9 17.6 %copy-start.7 = (f32[128]{0:T(128)S(1)}, f32[128]{0:T(128)}, u32[]{:S(2)}) copy-start(f32[128]{0:T(128)} %param.21) | copy-start | bytes 1540
  30.8 13.7 %collective-permute-start.8 = (bf16[2,10,32,128]{3,2,1,0:T(8,128)(2,1)S(1)}, bf16[2,10,32,128]{3,2,1,0:T(8,128)(2,1)S(1)}, u32[]{:S(2)}, u32[]{:S(2)}) collective-permute-start(bf16[2,10,32,128]{3,2,1,0:T(8,128)(2,1)S(1)} %get-tuple-element.21), channel_id=1, source_target_pairs={{0,2},{1,3},{2,4},{3,5},{4,6},{5,7},{6,8},{7,9},{8,10},{9,11},{10,... | collective-permute-start | bytes 491528 | tf_op jit(solution)/shard_map/ppermute | solution.py:313
  43.3 1.2 %collective-permute-start.9 = (f32[16,2,128]{2,1,0:T(2,128)S(1)}, f32[16,2,128]{2,1,0:T(2,128)S(1)}, u32[]{:S(2)}, u32[]{:S(2)}) collective-permute-start(f32[16,2,128]{2,1,0:T(2,128)S(1)} %all_to_all.10.moments_ref), channel_id=1, source_target_pairs={{0,16},{16,0},{1,17},{17,1},{2,18},{18,2},{3,19},{19,3},{4,20},{20... | collective-permute-start | bytes 49160 | tf_op jit(solution)/shard_map/ppermute | solution.py:316
